TPU v7x, 32 devices: a whole 2x2x4 slice. The times are simulated.
32 devices in a mesh: groups: 1, store: 32 (over z, y, x, core).
Axes of the slice: x: 2, y: 2, z: 4, core: 2. Of those that a mesh axis runs over, the one named last changes fastest.
Arguments:
- span_kv: bfloat16 [64, 512, 256], P(('groups', 'store')), may hold values from -6 to 6
- span_home: int32 [8], P('groups'), may hold values from 0 to 7, each once
- request_spans: int32 [32, 4], P('groups'), may hold values from 0 to 7, all different within a row
- recomp_pos: int32 [32, 4, 32], P('groups'), may hold values from 0 to 511, as said below
- new_q: bfloat16 [256, 130, 1024], P(('groups', 'store'))
- new_kv: bfloat16 [256, 130, 256], P(('groups', 'store'))
Outputs:
- attended: bfloat16 [256, 130, 1024], P(('groups', 'store'))
Inputs may be any that keep to these rules, and one draw needn't show every extreme that they name: `span_home`: each span id is stored in exactly one slot. `request_spans`: a request names 4 different spans. `recomp_pos`: strictly increasing along the last dimension.
All inputs are finite; a program needn't handle non-finite values.
Results may differ from a plain program's by a relative error of at most 0.0087.
Values may be sent and summed in bfloat16 or wider, within the bound.
No kernel may reach another device: no remote copies, remote signals or barrier semaphores. Data moves between devices by JAX's collectives and lax.ppermute only.
A program may use at most 128 MiB of HBM per device.

v0:
```python
import jax
import jax.numpy as jnp
from jax import lax
from jax.sharding import PartitionSpec as P

KV_HEADS = 8


def shifted(value, axis, by):
    devices = lax.axis_size(axis)
    return lax.ppermute(value, axis, [(i, (i + by) % devices) for i in range(devices)])


def rope_table(positions, half_dim):
    frequency = jnp.exp(
        -(2.0 * jnp.arange(half_dim).astype(jnp.float32) / (2.0 * half_dim))
        * jnp.log(jnp.float32(500000.0))
    )
    angles = positions.astype(jnp.float32)[..., None] * frequency
    return (jnp.cos(angles), jnp.sin(angles))


def rotate(source_rows, cosines, sines):
    half_dim = source_rows.shape[-1] // 2
    front_half = source_rows[..., :half_dim]
    back_half = source_rows[..., half_dim:]
    return jnp.concatenate(
        [front_half * cosines - back_half * sines, back_half * cosines + front_half * sines], -1
    )


def attend(cached, queries, fresh, offsets):
    joined_count, length, row_width = cached.shape
    head_dim = row_width // 2
    row_count = queries.shape[0]
    recomputed = joined_count * offsets.shape[1]
    decode_count = row_count - recomputed
    bases = jnp.arange(joined_count, dtype=jnp.int32) * length
    cosines, sines = rope_table(bases, head_dim // 2)
    key_rows = rotate(
        cached[..., :head_dim].astype(jnp.float32), cosines[:, None, :], sines[:, None, :]
    )
    key_rows = key_rows.astype(jnp.bfloat16).reshape(joined_count * length, head_dim)
    value_rows = cached[..., head_dim:].reshape(joined_count * length, head_dim)
    places = (offsets + bases[:, None]).reshape(-1)
    row_pos = jnp.concatenate(
        [places, joined_count * length + jnp.arange(decode_count, dtype=jnp.int32)]
    )
    row_cos, row_sin = rope_table(row_pos, head_dim // 2)
    fresh_keys = rotate(fresh[:, :head_dim].astype(jnp.float32), row_cos, row_sin).astype(
        jnp.bfloat16
    )
    fresh_values = fresh[:, head_dim:]
    key_rows = key_rows.at[places].set(fresh_keys[:recomputed])
    value_rows = value_rows.at[places].set(fresh_values[:recomputed])
    key_rows = jnp.concatenate([key_rows, fresh_keys[recomputed:]], 0)
    value_rows = jnp.concatenate([value_rows, fresh_values[recomputed:]], 0)
    head_count = queries.shape[1] // head_dim
    query_rows = queries.reshape(row_count, head_count, head_dim).astype(jnp.float32)
    query_rows = rotate(query_rows, row_cos[:, None, :], row_sin[:, None, :]).astype(jnp.bfloat16)
    scores = jnp.einsum(
        "rhd,kd->hrk", query_rows, key_rows, preferred_element_type=jnp.float32
    ) / jnp.sqrt(jnp.float32(head_dim))
    key_pos = jnp.arange(key_rows.shape[0], dtype=jnp.int32)
    visible = key_pos[None, None, :] <= row_pos[None, :, None]
    scores = jnp.where(visible, scores, jnp.float32(-1e30))
    peaks = jnp.max(scores, -1, keepdims=True)
    powers = jnp.where(visible, jnp.exp(scores - peaks), jnp.float32(0.0))
    totals = jnp.sum(powers, -1, keepdims=True)
    weights = (powers / totals).astype(jnp.bfloat16)
    output = jnp.einsum("hrk,kd->rhd", weights, value_rows, preferred_element_type=jnp.float32)
    return output.reshape(row_count, head_count * head_dim).astype(jnp.bfloat16)


def local(span_kv, span_home, request_spans, recomp_pos, new_q, new_kv):
    group_count = lax.axis_size("store") // KV_HEADS
    device_index = lax.axis_index("store")
    store_group = device_index // KV_HEADS
    slot_count = span_kv.shape[0]
    gathered = jnp.zeros((group_count * slot_count,) + span_kv.shape[1:], jnp.bfloat16)
    gathered = lax.dynamic_update_slice_in_dim(gathered, span_kv, store_group * slot_count, 0)

    def advance(section, carry):
        moving, collected = carry
        moving = shifted(moving, "store", KV_HEADS)
        root = (store_group - section) % group_count
        collected = lax.dynamic_update_slice_in_dim(collected, moving, root * slot_count, 0)
        return (moving, collected)

    _, gathered = lax.fori_loop(1, group_count, advance, (span_kv, gathered))
    local_count = new_q.shape[0]

    def single(member):
        request = store_group * local_count + member
        span_slots = span_home[request_spans[request]]
        cached = gathered[span_slots]
        return attend(cached, new_q[member], new_kv[member], recomp_pos[request])

    return lax.map(single, jnp.arange(local_count, dtype=jnp.int32))


def solution(mesh):
    return jax.shard_map(
        local,
        mesh=mesh,
        in_specs=(
            P(("groups", "store"), None, None),
            P("groups"),
            P("groups", None),
            P("groups", None, None),
            P(("groups", "store"), None, None),
            P(("groups", "store"), None, None),
        ),
        out_specs=P(("groups", "store"), None, None),
        check_vma=False,
    )
```

profile of v0, /device:TPU:0, one launch (start us, length us, event | category | flops | bytes accessed | tf_op | source)
XLA Modules:
  0.0 317.8 jit_solution(403666200891015915)
XLA Ops:
  0.0 1.0 copy.53
  1.8 2.0 copy.14
  4.0 46.3 %while.29 = (s32[]{:T(128)}, bf16[2,512,256]{2,1,0:T(8,128)(2,1)S(1)}, bf16[8,512,256]{2,1,0:T(8,128)(2,1)S(1)}, s32[]{:T(128)}, s32[]{:T(128)}, /*index=5*/s32[...) while((s32[]{:T(128)}, bf16[2,512,256]{2,1,0:T(8,128)(2,1)S(1)}, bf16[8,512,256]{2,1,0:T(8,128)(2,1)S(1)}, ...), condition=%wide.region_1.2_spmd, body=%wide.region_0.1_spmd.sunk | while | flops 18 | bytes 4194616 | solution.py:90
  4.0 3.1 collective-permute-start
  7.0 13.9 %collective-permute-done = bf16[2,512,256]{2,1,0:T(8,128)(2,1)S(1)} collective-permute-done((bf16[2,512,256]{2,1,0:T(8,128)(2,1)S(1)}, bf16[2,512,256]{2,1,0:T(8,128)(2,1)S(1)}, u32[]{:S(2)}, u32[]{:S(2)}) %collective-permute-start) | collective-permute-done | bytes 524320 | tf_op jit(solution)/shard_map/while/body/eval_jaxpr/ppermute | solution.py:11
  21.2 14.9 %collective-permute-done = bf16[2,512,256]{2,1,0:T(8,128)(2,1)S(1)} collective-permute-done((bf16[2,512,256]{2,1,0:T(8,128)(2,1)S(1)}, bf16[2,512,256]{2,1,0:T(8,128)(2,1)S(1)}, u32[]{:S(2)}, u32[]{:S(2)}) %collective-permute-start) | collective-permute-done | bytes 524320 | tf_op jit(solution)/shard_map/while/body/eval_jaxpr/ppermute | solution.py:11
  36.2 13.9 %collective-permute-done = bf16[2,512,256]{2,1,0:T(8,128)(2,1)S(1)} collective-permute-done((bf16[2,512,256]{2,1,0:T(8,128)(2,1)S(1)}, bf16[2,512,256]{2,1,0:T(8,128)(2,1)S(1)}, u32[]{:S(2)}, u32[]{:S(2)}) %collective-permute-start) | collective-permute-done | bytes 524320 | tf_op jit(solution)/shard_map/while/body/eval_jaxpr/ppermute | solution.py:11
  50.3 4.1 %copy.15 = bf16[8,130,1024]{2,1,0:T(8,128)(2,1)} copy(bf16[8,130,1024]{2,0,1:T(8,128)(2,1)} %param.14) | data formatting | bytes 4259840 | tf_op jit(solution)/shard_map/while | solution.py:99
  54.4 259.2 %while.30 = (s32[]{:T(128)}, bf16[8,130,1024]{2,1,0:T(8,128)(2,1)}, s32[8]{0:T(128)S(1)}, s32[]{:T(128)}, s32[32,4]{1,0:T(8,128)S(1)}, /*index=5*/s32[8]{0:T(128...) while((s32[]{:T(128)}, bf16[8,130,1024]{2,1,0:T(8,128)(2,1)}, ...), condition=%wide.region_7.8_spmd, body=%wide.region_2.7_spmd.sunk | while | flops 1114038656 | bytes 35693692 | solution.py:99
  63.9 1.0 dynamic-slice_convert_fusion.2
  65.2 1.0 subtract_convert_fusion.6
  67.0 0.9 fusion.66
  68.7 1.5 scatter_custom_fusion.10
  70.3 1.3 scatter_custom_fusion.11
  71.6 9.1 %fusion.70 = (f32[8,130]{1,0:T(8,128)S(1)}, f32[8,130,2050]{2,1,0:T(8,128)}) fusion(pred[130,2050]{1,0:T(8,128)(4,1)S(1)} %iota_compare_fusion.3, bf16[130,64]{1,0:T(8,128)(2,1)S(1)} %get-tuple-element.419, bf16[130,64]{1,0:T(8,128)(2,1)} %get-tuple-element.420, bf16[2048,128]{1,0:T(8,128)(2,1)S(1)} %scatter_custom_fusion.10, ...), kind=kOutput, calls=%fused_computation.78.clone.1 | convolution fusion | flops 559347968 | bytes 9622468 | tf_op jit(solution)/shard_map/while/body/eval_jaxpr/sub | solution.py:68
  80.8 5.1 %fusion.71 = bf16[130,8,128]{2,0,1:T(8,128)(2,1)S(1)} fusion(f32[8,130,2050]{2,1,0:T(8,128)} %get-tuple-element.432, f32[8,130]{1,0:T(8,128)S(1)} %get-tuple-element.433, bf16[2,128]{1,0:T(2,128)(2,1)S(1)} %copy-done.8, bf16[2048,128]{1,0:T(8,128)(2,1)S(1)} %scatter_custom_fusion.11), kind=kOutput, calls=%fused_computation.17.clone.1 | convolution fusion | flops 551238720 | bytes 9323200 | tf_op jit(solution)/shard_map/while/body/eval_jaxpr/hrk,kd->rhd/dot_general | solution.py:71
  96.3 1.0 dynamic-slice_convert_fusion.2
  97.6 1.0 subtract_convert_fusion.6
  99.4 0.9 fusion.66
  101.1 1.5 scatter_custom_fusion.10
  102.7 1.3 scatter_custom_fusion.11
  104.0 9.1 %fusion.70 = (f32[8,130]{1,0:T(8,128)S(1)}, f32[8,130,2050]{2,1,0:T(8,128)}) fusion(pred[130,2050]{1,0:T(8,128)(4,1)S(1)} %iota_compare_fusion.3, bf16[130,64]{1,0:T(8,128)(2,1)S(1)} %get-tuple-element.419, bf16[130,64]{1,0:T(8,128)(2,1)} %get-tuple-element.420, bf16[2048,128]{1,0:T(8,128)(2,1)S(1)} %scatter_custom_fusion.10, ...), kind=kOutput, calls=%fused_computation.78.clone.1 | convolution fusion | flops 559347968 | bytes 9622468 | tf_op jit(solution)/shard_map/while/body/eval_jaxpr/sub | solution.py:68
  113.2 5.1 %fusion.71 = bf16[130,8,128]{2,0,1:T(8,128)(2,1)S(1)} fusion(f32[8,130,2050]{2,1,0:T(8,128)} %get-tuple-element.432, f32[8,130]{1,0:T(8,128)S(1)} %get-tuple-element.433, bf16[2,128]{1,0:T(2,128)(2,1)S(1)} %copy-done.8, bf16[2048,128]{1,0:T(8,128)(2,1)S(1)} %scatter_custom_fusion.11), kind=kOutput, calls=%fused_computation.17.clone.1 | convolution fusion | flops 551238720 | bytes 9323200 | tf_op jit(solution)/shard_map/while/body/eval_jaxpr/hrk,kd->rhd/dot_general | solution.py:71
  128.7 1.0 dynamic-slice_convert_fusion.2
  130.0 1.0 subtract_convert_fusion.6
  131.8 0.9 fusion.66
  133.5 1.5 scatter_custom_fusion.10
  135.0 1.3 scatter_custom_fusion.11
  136.4 9.1 %fusion.70 = (f32[8,130]{1,0:T(8,128)S(1)}, f32[8,130,2050]{2,1,0:T(8,128)}) fusion(pred[130,2050]{1,0:T(8,128)(4,1)S(1)} %iota_compare_fusion.3, bf16[130,64]{1,0:T(8,128)(2,1)S(1)} %get-tuple-element.419, bf16[130,64]{1,0:T(8,128)(2,1)} %get-tuple-element.420, bf16[2048,128]{1,0:T(8,128)(2,1)S(1)} %scatter_custom_fusion.10, ...), kind=kOutput, calls=%fused_computation.78.clone.1 | convolution fusion | flops 559347968 | bytes 9622468 | tf_op jit(solution)/shard_map/while/body/eval_jaxpr/sub | solution.py:68
  145.5 5.1 %fusion.71 = bf16[130,8,128]{2,0,1:T(8,128)(2,1)S(1)} fusion(f32[8,130,2050]{2,1,0:T(8,128)} %get-tuple-element.432, f32[8,130]{1,0:T(8,128)S(1)} %get-tuple-element.433, bf16[2,128]{1,0:T(2,128)(2,1)S(1)} %copy-done.8, bf16[2048,128]{1,0:T(8,128)(2,1)S(1)} %scatter_custom_fusion.11), kind=kOutput, calls=%fused_computation.17.clone.1 | convolution fusion | flops 551238720 | bytes 9323200 | tf_op jit(solution)/shard_map/while/body/eval_jaxpr/hrk,kd->rhd/dot_general | solution.py:71
  161.1 1.0 dynamic-slice_convert_fusion.2
  162.4 1.0 subtract_convert_fusion.6
  165.9 1.5 scatter_custom_fusion.10
  167.4 1.3 scatter_custom_fusion.11
  168.8 9.1 %fusion.70 = (f32[8,130]{1,0:T(8,128)S(1)}, f32[8,130,2050]{2,1,0:T(8,128)}) fusion(pred[130,2050]{1,0:T(8,128)(4,1)S(1)} %iota_compare_fusion.3, bf16[130,64]{1,0:T(8,128)(2,1)S(1)} %get-tuple-element.419, bf16[130,64]{1,0:T(8,128)(2,1)} %get-tuple-element.420, bf16[2048,128]{1,0:T(8,128)(2,1)S(1)} %scatter_custom_fusion.10, ...), kind=kOutput, calls=%fused_computation.78.clone.1 | convolution fusion | flops 559347968 | bytes 9622468 | tf_op jit(solution)/shard_map/while/body/eval_jaxpr/sub | solution.py:68
  178.0 5.1 %fusion.71 = bf16[130,8,128]{2,0,1:T(8,128)(2,1)S(1)} fusion(f32[8,130,2050]{2,1,0:T(8,128)} %get-tuple-element.432, f32[8,130]{1,0:T(8,128)S(1)} %get-tuple-element.433, bf16[2,128]{1,0:T(2,128)(2,1)S(1)} %copy-done.8, bf16[2048,128]{1,0:T(8,128)(2,1)S(1)} %scatter_custom_fusion.11), kind=kOutput, calls=%fused_computation.17.clone.1 | convolution fusion | flops 551238720 | bytes 9323200 | tf_op jit(solution)/shard_map/while/body/eval_jaxpr/hrk,kd->rhd/dot_general | solution.py:71
  193.5 1.0 dynamic-slice_convert_fusion.2
  194.8 1.0 subtract_convert_fusion.6
  196.6 0.9 fusion.66
  198.3 1.5 scatter_custom_fusion.10
  199.9 1.3 scatter_custom_fusion.11
  201.2 9.1 %fusion.70 = (f32[8,130]{1,0:T(8,128)S(1)}, f32[8,130,2050]{2,1,0:T(8,128)}) fusion(pred[130,2050]{1,0:T(8,128)(4,1)S(1)} %iota_compare_fusion.3, bf16[130,64]{1,0:T(8,128)(2,1)S(1)} %get-tuple-element.419, bf16[130,64]{1,0:T(8,128)(2,1)} %get-tuple-element.420, bf16[2048,128]{1,0:T(8,128)(2,1)S(1)} %scatter_custom_fusion.10, ...), kind=kOutput, calls=%fused_computation.78.clone.1 | convolution fusion | flops 559347968 | bytes 9622468 | tf_op jit(solution)/shard_map/while/body/eval_jaxpr/sub | solution.py:68
  210.4 5.1 %fusion.71 = bf16[130,8,128]{2,0,1:T(8,128)(2,1)S(1)} fusion(f32[8,130,2050]{2,1,0:T(8,128)} %get-tuple-element.432, f32[8,130]{1,0:T(8,128)S(1)} %get-tuple-element.433, bf16[2,128]{1,0:T(2,128)(2,1)S(1)} %copy-done.8, bf16[2048,128]{1,0:T(8,128)(2,1)S(1)} %scatter_custom_fusion.11), kind=kOutput, calls=%fused_computation.17.clone.1 | convolution fusion | flops 551238720 | bytes 9323200 | tf_op jit(solution)/shard_map/while/body/eval_jaxpr/hrk,kd->rhd/dot_general | solution.py:71
  225.9 1.0 dynamic-slice_convert_fusion.2
  227.2 1.0 subtract_convert_fusion.6
  230.7 1.5 scatter_custom_fusion.10
  232.3 1.3 scatter_custom_fusion.11
  233.6 9.1 %fusion.70 = (f32[8,130]{1,0:T(8,128)S(1)}, f32[8,130,2050]{2,1,0:T(8,128)}) fusion(pred[130,2050]{1,0:T(8,128)(4,1)S(1)} %iota_compare_fusion.3, bf16[130,64]{1,0:T(8,128)(2,1)S(1)} %get-tuple-element.419, bf16[130,64]{1,0:T(8,128)(2,1)} %get-tuple-element.420, bf16[2048,128]{1,0:T(8,128)(2,1)S(1)} %scatter_custom_fusion.10, ...), kind=kOutput, calls=%fused_computation.78.clone.1 | convolution fusion | flops 559347968 | bytes 9622468 | tf_op jit(solution)/shard_map/while/body/eval_jaxpr/sub | solution.py:68
  242.8 5.1 %fusion.71 = bf16[130,8,128]{2,0,1:T(8,128)(2,1)S(1)} fusion(f32[8,130,2050]{2,1,0:T(8,128)} %get-tuple-element.432, f32[8,130]{1,0:T(8,128)S(1)} %get-tuple-element.433, bf16[2,128]{1,0:T(2,128)(2,1)S(1)} %copy-done.8, bf16[2048,128]{1,0:T(8,128)(2,1)S(1)} %scatter_custom_fusion.11), kind=kOutput, calls=%fused_computation.17.clone.1 | convolution fusion | flops 551238720 | bytes 9323200 | tf_op jit(solution)/shard_map/while/body/eval_jaxpr/hrk,kd->rhd/dot_general | solution.py:71
  258.3 1.0 dynamic-slice_convert_fusion.2
  259.7 1.0 subtract_convert_fusion.6
  261.4 0.9 fusion.66
  263.1 1.5 scatter_custom_fusion.10
  264.7 1.3 scatter_custom_fusion.11
  266.0 9.1 %fusion.70 = (f32[8,130]{1,0:T(8,128)S(1)}, f32[8,130,2050]{2,1,0:T(8,128)}) fusion(pred[130,2050]{1,0:T(8,128)(4,1)S(1)} %iota_compare_fusion.3, bf16[130,64]{1,0:T(8,128)(2,1)S(1)} %get-tuple-element.419, bf16[130,64]{1,0:T(8,128)(2,1)} %get-tuple-element.420, bf16[2048,128]{1,0:T(8,128)(2,1)S(1)} %scatter_custom_fusion.10, ...), kind=kOutput, calls=%fused_computation.78.clone.1 | convolution fusion | flops 559347968 | bytes 9622468 | tf_op jit(solution)/shard_map/while/body/eval_jaxpr/sub | solution.py:68
  275.2 5.1 %fusion.71 = bf16[130,8,128]{2,0,1:T(8,128)(2,1)S(1)} fusion(f32[8,130,2050]{2,1,0:T(8,128)} %get-tuple-element.432, f32[8,130]{1,0:T(8,128)S(1)} %get-tuple-element.433, bf16[2,128]{1,0:T(2,128)(2,1)S(1)} %copy-done.8, bf16[2048,128]{1,0:T(8,128)(2,1)S(1)} %scatter_custom_fusion.11), kind=kOutput, calls=%fused_computation.17.clone.1 | convolution fusion | flops 551238720 | bytes 9323200 | tf_op jit(solution)/shard_map/while/body/eval_jaxpr/hrk,kd->rhd/dot_general | solution.py:71
  290.7 1.0 dynamic-slice_convert_fusion.2
  292.1 1.0 subtract_convert_fusion.6
  293.8 0.9 fusion.66
  295.5 1.5 scatter_custom_fusion.10
  297.1 1.3 scatter_custom_fusion.11
  298.4 9.1 %fusion.70 = (f32[8,130]{1,0:T(8,128)S(1)}, f32[8,130,2050]{2,1,0:T(8,128)}) fusion(pred[130,2050]{1,0:T(8,128)(4,1)S(1)} %iota_compare_fusion.3, bf16[130,64]{1,0:T(8,128)(2,1)S(1)} %get-tuple-element.419, bf16[130,64]{1,0:T(8,128)(2,1)} %get-tuple-element.420, bf16[2048,128]{1,0:T(8,128)(2,1)S(1)} %scatter_custom_fusion.10, ...), kind=kOutput, calls=%fused_computation.78.clone.1 | convolution fusion | flops 559347968 | bytes 9622468 | tf_op jit(solution)/shard_map/while/body/eval_jaxpr/sub | solution.py:68
  307.6 5.1 %fusion.71 = bf16[130,8,128]{2,0,1:T(8,128)(2,1)S(1)} fusion(f32[8,130,2050]{2,1,0:T(8,128)} %get-tuple-element.432, f32[8,130]{1,0:T(8,128)S(1)} %get-tuple-element.433, bf16[2,128]{1,0:T(2,128)(2,1)S(1)} %copy-done.8, bf16[2048,128]{1,0:T(8,128)(2,1)S(1)} %scatter_custom_fusion.11), kind=kOutput, calls=%fused_computation.17.clone.1 | convolution fusion | flops 551238720 | bytes 9323200 | tf_op jit(solution)/shard_map/while/body/eval_jaxpr/hrk,kd->rhd/dot_general | solution.py:71
  313.6 4.1 %copy.16 = bf16[8,130,1024]{2,0,1:T(8,128)(2,1)} copy(bf16[8,130,1024]{2,1,0:T(8,128)(2,1)} %get-tuple-element.244) | data formatting | bytes 4259840 | tf_op jit(solution)/shard_map/while | solution.py:99
  (409 shorter events, 79.7 us)
Async XLA Ops:
  4.0 17.0 %collective-permute-start = (bf16[2,512,256]{2,1,0:T(8,128)(2,1)S(1)}, bf16[2,512,256]{2,1,0:T(8,128)(2,1)S(1)}, u32[]{:S(2)}, u32[]{:S(2)}) collective-permute-start(bf16[2,512,256]{2,1,0:T(8,128)(2,1)S(1)} %get-tuple-element.446), channel_id=1, source_target_pairs={{0,8},{1,9},{2,10},{3,11},{4,12},{5,13},{6,14},{7,15},{8,16},{9,17... | collective-permute-start | bytes 1572872 | tf_op jit(solution)/shard_map/while/body/eval_jaxpr/ppermute | solution.py:11
  21.1 15.0 %collective-permute-start = (bf16[2,512,256]{2,1,0:T(8,128)(2,1)S(1)}, bf16[2,512,256]{2,1,0:T(8,128)(2,1)S(1)}, u32[]{:S(2)}, u32[]{:S(2)}) collective-permute-start(bf16[2,512,256]{2,1,0:T(8,128)(2,1)S(1)} %get-tuple-element.446), channel_id=1, source_target_pairs={{0,8},{1,9},{2,10},{3,11},{4,12},{5,13},{6,14},{7,15},{8,16},{9,17... | collective-permute-start | bytes 1572872 | tf_op jit(solution)/shard_map/while/body/eval_jaxpr/ppermute | solution.py:11
  36.1 14.0 %collective-permute-start = (bf16[2,512,256]{2,1,0:T(8,128)(2,1)S(1)}, bf16[2,512,256]{2,1,0:T(8,128)(2,1)S(1)}, u32[]{:S(2)}, u32[]{:S(2)}) collective-permute-start(bf16[2,512,256]{2,1,0:T(8,128)(2,1)S(1)} %get-tuple-element.446), channel_id=1, source_target_pairs={{0,8},{1,9},{2,10},{3,11},{4,12},{5,13},{6,14},{7,15},{8,16},{9,17... | collective-permute-start | bytes 1572872 | tf_op jit(solution)/shard_map/while/body/eval_jaxpr/ppermute | solution.py:11
  50.3 4.1 %copy-start = (s32[8]{0:T(128)S(1)}, s32[8]{0:T(128)}, u32[]{:S(2)}) copy-start(s32[8]{0:T(128)} %param.11) | copy-start | bytes 100
  54.4 10.8 %copy-start.4 = (s32[32,4]{1,0:T(8,128)}, s32[32,4]{1,0:T(8,128)S(1)}, u32[]{:S(2)}) copy-start(s32[32,4]{1,0:T(8,128)S(1)} %get-tuple-element.499) | copy-start | bytes 1540 | tf_op jit(solution)/shard_map/while
  54.4 10.8 %copy-start.6 = (s32[8]{0:T(128)}, s32[8]{0:T(128)S(1)}, u32[]{:S(2)}) copy-start(s32[8]{0:T(128)S(1)} %get-tuple-element.497) | copy-start | bytes 100 | tf_op jit(solution)/shard_map/while
  67.0 1.0 copy-start.2
  67.0 1.0 copy-start.3
  68.0 2.3 copy-start.1
  71.6 9.2 %copy-start.8 = (bf16[2,128]{1,0:T(2,128)(2,1)S(1)}, bf16[2,128]{1,0:T(2,128)(2,1)}, u32[]{:S(2)}) copy-start(bf16[2,128]{1,0:T(2,128)(2,1)} %slice.147) | copy-start | bytes 1540 | tf_op jit(solution)/shard_map/while
  80.8 6.1 %copy-start.5 = (s32[32,4]{1,0:T(8,128)S(1)}, s32[32,4]{1,0:T(8,128)}, u32[]{:S(2)}) copy-start(s32[32,4]{1,0:T(8,128)} %copy-done.4) | copy-start | bytes 1540 | tf_op jit(solution)/shard_map/while
  80.8 6.1 %copy-start.7 = (s32[8]{0:T(128)S(1)}, s32[8]{0:T(128)}, u32[]{:S(2)}) copy-start(s32[8]{0:T(128)} %copy-done.6) | copy-start | bytes 100 | tf_op jit(solution)/shard_map/while
  86.8 10.8 %copy-start.4 = (s32[32,4]{1,0:T(8,128)}, s32[32,4]{1,0:T(8,128)S(1)}, u32[]{:S(2)}) copy-start(s32[32,4]{1,0:T(8,128)S(1)} %get-tuple-element.499) | copy-start | bytes 1540 | tf_op jit(solution)/shard_map/while
  86.8 10.8 %copy-start.6 = (s32[8]{0:T(128)}, s32[8]{0:T(128)S(1)}, u32[]{:S(2)}) copy-start(s32[8]{0:T(128)S(1)} %get-tuple-element.497) | copy-start | bytes 100 | tf_op jit(solution)/shard_map/while
  99.4 1.0 copy-start.2
  99.4 1.0 copy-start.3
  100.4 2.3 copy-start.1
  104.0 9.2 %copy-start.8 = (bf16[2,128]{1,0:T(2,128)(2,1)S(1)}, bf16[2,128]{1,0:T(2,128)(2,1)}, u32[]{:S(2)}) copy-start(bf16[2,128]{1,0:T(2,128)(2,1)} %slice.147) | copy-start | bytes 1540 | tf_op jit(solution)/shard_map/while
  113.2 6.1 %copy-start.5 = (s32[32,4]{1,0:T(8,128)S(1)}, s32[32,4]{1,0:T(8,128)}, u32[]{:S(2)}) copy-start(s32[32,4]{1,0:T(8,128)} %copy-done.4) | copy-start | bytes 1540 | tf_op jit(solution)/shard_map/while
  113.2 6.1 %copy-start.7 = (s32[8]{0:T(128)S(1)}, s32[8]{0:T(128)}, u32[]{:S(2)}) copy-start(s32[8]{0:T(128)} %copy-done.6) | copy-start | bytes 100 | tf_op jit(solution)/shard_map/while
  119.2 10.8 %copy-start.4 = (s32[32,4]{1,0:T(8,128)}, s32[32,4]{1,0:T(8,128)S(1)}, u32[]{:S(2)}) copy-start(s32[32,4]{1,0:T(8,128)S(1)} %get-tuple-element.499) | copy-start | bytes 1540 | tf_op jit(solution)/shard_map/while
  119.2 10.8 %copy-start.6 = (s32[8]{0:T(128)}, s32[8]{0:T(128)S(1)}, u32[]{:S(2)}) copy-start(s32[8]{0:T(128)S(1)} %get-tuple-element.497) | copy-start | bytes 100 | tf_op jit(solution)/shard_map/while
  131.8 1.0 copy-start.2
  131.8 1.0 copy-start.3
  132.8 2.3 copy-start.1
  136.4 9.1 %copy-start.8 = (bf16[2,128]{1,0:T(2,128)(2,1)S(1)}, bf16[2,128]{1,0:T(2,128)(2,1)}, u32[]{:S(2)}) copy-start(bf16[2,128]{1,0:T(2,128)(2,1)} %slice.147) | copy-start | bytes 1540 | tf_op jit(solution)/shard_map/while
  145.5 6.1 %copy-start.5 = (s32[32,4]{1,0:T(8,128)S(1)}, s32[32,4]{1,0:T(8,128)}, u32[]{:S(2)}) copy-start(s32[32,4]{1,0:T(8,128)} %copy-done.4) | copy-start | bytes 1540 | tf_op jit(solution)/shard_map/while
  145.5 6.1 %copy-start.7 = (s32[8]{0:T(128)S(1)}, s32[8]{0:T(128)}, u32[]{:S(2)}) copy-start(s32[8]{0:T(128)} %copy-done.6) | copy-start | bytes 100 | tf_op jit(solution)/shard_map/while
  151.6 10.8 %copy-start.4 = (s32[32,4]{1,0:T(8,128)}, s32[32,4]{1,0:T(8,128)S(1)}, u32[]{:S(2)}) copy-start(s32[32,4]{1,0:T(8,128)S(1)} %get-tuple-element.499) | copy-start | bytes 1540 | tf_op jit(solution)/shard_map/while
  151.6 10.8 %copy-start.6 = (s32[8]{0:T(128)}, s32[8]{0:T(128)S(1)}, u32[]{:S(2)}) copy-start(s32[8]{0:T(128)S(1)} %get-tuple-element.497) | copy-start | bytes 100 | tf_op jit(solution)/shard_map/while
  164.2 1.0 copy-start.2
  165.2 2.3 copy-start.1
  168.8 9.2 %copy-start.8 = (bf16[2,128]{1,0:T(2,128)(2,1)S(1)}, bf16[2,128]{1,0:T(2,128)(2,1)}, u32[]{:S(2)}) copy-start(bf16[2,128]{1,0:T(2,128)(2,1)} %slice.147) | copy-start | bytes 1540 | tf_op jit(solution)/shard_map/while
  177.9 6.1 %copy-start.5 = (s32[32,4]{1,0:T(8,128)S(1)}, s32[32,4]{1,0:T(8,128)}, u32[]{:S(2)}) copy-start(s32[32,4]{1,0:T(8,128)} %copy-done.4) | copy-start | bytes 1540 | tf_op jit(solution)/shard_map/while
  177.9 6.1 %copy-start.7 = (s32[8]{0:T(128)S(1)}, s32[8]{0:T(128)}, u32[]{:S(2)}) copy-start(s32[8]{0:T(128)} %copy-done.6) | copy-start | bytes 100 | tf_op jit(solution)/shard_map/while
  184.0 10.8 %copy-start.4 = (s32[32,4]{1,0:T(8,128)}, s32[32,4]{1,0:T(8,128)S(1)}, u32[]{:S(2)}) copy-start(s32[32,4]{1,0:T(8,128)S(1)} %get-tuple-element.499) | copy-start | bytes 1540 | tf_op jit(solution)/shard_map/while
  184.0 10.8 %copy-start.6 = (s32[8]{0:T(128)}, s32[8]{0:T(128)S(1)}, u32[]{:S(2)}) copy-start(s32[8]{0:T(128)S(1)} %get-tuple-element.497) | copy-start | bytes 100 | tf_op jit(solution)/shard_map/while
  196.6 1.0 copy-start.2
  196.6 1.0 copy-start.3
  197.6 2.3 copy-start.1
  201.2 9.1 %copy-start.8 = (bf16[2,128]{1,0:T(2,128)(2,1)S(1)}, bf16[2,128]{1,0:T(2,128)(2,1)}, u32[]{:S(2)}) copy-start(bf16[2,128]{1,0:T(2,128)(2,1)} %slice.147) | copy-start | bytes 1540 | tf_op jit(solution)/shard_map/while
  210.3 6.1 %copy-start.5 = (s32[32,4]{1,0:T(8,128)S(1)}, s32[32,4]{1,0:T(8,128)}, u32[]{:S(2)}) copy-start(s32[32,4]{1,0:T(8,128)} %copy-done.4) | copy-start | bytes 1540 | tf_op jit(solution)/shard_map/while
  210.4 6.1 %copy-start.7 = (s32[8]{0:T(128)S(1)}, s32[8]{0:T(128)}, u32[]{:S(2)}) copy-start(s32[8]{0:T(128)} %copy-done.6) | copy-start | bytes 100 | tf_op jit(solution)/shard_map/while
  216.4 10.8 %copy-start.4 = (s32[32,4]{1,0:T(8,128)}, s32[32,4]{1,0:T(8,128)S(1)}, u32[]{:S(2)}) copy-start(s32[32,4]{1,0:T(8,128)S(1)} %get-tuple-element.499) | copy-start | bytes 1540 | tf_op jit(solution)/shard_map/while
  216.4 10.8 %copy-start.6 = (s32[8]{0:T(128)}, s32[8]{0:T(128)S(1)}, u32[]{:S(2)}) copy-start(s32[8]{0:T(128)S(1)} %get-tuple-element.497) | copy-start | bytes 100 | tf_op jit(solution)/shard_map/while
  229.0 1.0 copy-start.2
  230.0 2.3 copy-start.1
  233.6 9.2 %copy-start.8 = (bf16[2,128]{1,0:T(2,128)(2,1)S(1)}, bf16[2,128]{1,0:T(2,128)(2,1)}, u32[]{:S(2)}) copy-start(bf16[2,128]{1,0:T(2,128)(2,1)} %slice.147) | copy-start | bytes 1540 | tf_op jit(solution)/shard_map/while
  242.8 6.1 %copy-start.5 = (s32[32,4]{1,0:T(8,128)S(1)}, s32[32,4]{1,0:T(8,128)}, u32[]{:S(2)}) copy-start(s32[32,4]{1,0:T(8,128)} %copy-done.4) | copy-start | bytes 1540 | tf_op jit(solution)/shard_map/while
  242.8 6.1 %copy-start.7 = (s32[8]{0:T(128)S(1)}, s32[8]{0:T(128)}, u32[]{:S(2)}) copy-start(s32[8]{0:T(128)} %copy-done.6) | copy-start | bytes 100 | tf_op jit(solution)/shard_map/while
  248.9 10.8 %copy-start.4 = (s32[32,4]{1,0:T(8,128)}, s32[32,4]{1,0:T(8,128)S(1)}, u32[]{:S(2)}) copy-start(s32[32,4]{1,0:T(8,128)S(1)} %get-tuple-element.499) | copy-start | bytes 1540 | tf_op jit(solution)/shard_map/while
  248.9 10.8 %copy-start.6 = (s32[8]{0:T(128)}, s32[8]{0:T(128)S(1)}, u32[]{:S(2)}) copy-start(s32[8]{0:T(128)S(1)} %get-tuple-element.497) | copy-start | bytes 100 | tf_op jit(solution)/shard_map/while
  261.4 1.0 copy-start.2
  262.4 2.3 copy-start.1
  266.0 9.2 %copy-start.8 = (bf16[2,128]{1,0:T(2,128)(2,1)S(1)}, bf16[2,128]{1,0:T(2,128)(2,1)}, u32[]{:S(2)}) copy-start(bf16[2,128]{1,0:T(2,128)(2,1)} %slice.147) | copy-start | bytes 1540 | tf_op jit(solution)/shard_map/while
  275.2 6.1 %copy-start.5 = (s32[32,4]{1,0:T(8,128)S(1)}, s32[32,4]{1,0:T(8,128)}, u32[]{:S(2)}) copy-start(s32[32,4]{1,0:T(8,128)} %copy-done.4) | copy-start | bytes 1540 | tf_op jit(solution)/shard_map/while
  275.2 6.1 %copy-start.7 = (s32[8]{0:T(128)S(1)}, s32[8]{0:T(128)}, u32[]{:S(2)}) copy-start(s32[8]{0:T(128)} %copy-done.6) | copy-start | bytes 100 | tf_op jit(solution)/shard_map/while
  281.2 10.8 %copy-start.4 = (s32[32,4]{1,0:T(8,128)}, s32[32,4]{1,0:T(8,128)S(1)}, u32[]{:S(2)}) copy-start(s32[32,4]{1,0:T(8,128)S(1)} %get-tuple-element.499) | copy-start | bytes 1540 | tf_op jit(solution)/shard_map/while
  281.3 10.8 %copy-start.6 = (s32[8]{0:T(128)}, s32[8]{0:T(128)S(1)}, u32[]{:S(2)}) copy-start(s32[8]{0:T(128)S(1)} %get-tuple-element.497) | copy-start | bytes 100 | tf_op jit(solution)/shard_map/while
  293.8 1.0 copy-start.2
  294.8 2.3 copy-start.1
  298.4 9.2 %copy-start.8 = (bf16[2,128]{1,0:T(2,128)(2,1)S(1)}, bf16[2,128]{1,0:T(2,128)(2,1)}, u32[]{:S(2)}) copy-start(bf16[2,128]{1,0:T(2,128)(2,1)} %slice.147) | copy-start | bytes 1540 | tf_op jit(solution)/shard_map/while
  307.6 6.1 %copy-start.5 = (s32[32,4]{1,0:T(8,128)S(1)}, s32[32,4]{1,0:T(8,128)}, u32[]{:S(2)}) copy-start(s32[32,4]{1,0:T(8,128)} %copy-done.4) | copy-start | bytes 1540 | tf_op jit(solution)/shard_map/while
  307.6 6.1 %copy-start.7 = (s32[8]{0:T(128)S(1)}, s32[8]{0:T(128)}, u32[]{:S(2)}) copy-start(s32[8]{0:T(128)} %copy-done.6) | copy-start | bytes 100 | tf_op jit(solution)/shard_map/while
  (4 other events, 3.8 us)
where the time goes:
time: 320 us; the launch traced here: 318 us
  matrix products  114 us (36%)
  local copies, waits for them, and re-layouts  69.4 us (22%)
  other arithmetic  66.2 us (21%)
  waiting for transfers between devices  42.8 us (13%)
  loops' own time  22 us (7%)
    sub x8, matrix products, attend(): powers = jnp.where(visible, jnp.exp(scores - peaks), jnp.float32(0.0))  73.1 us
    ppermute x3, waiting for transfers between devices, shifted(): lax.ppermute(value, axis, [(i, (i + by) % devices) for i in range(devices)])  42.8 us
    dot_general x8, matrix products, attend(): jnp.einsum('hrk,kd->rhd', weights, value_rows, preferred_element_type=jnp...  41.1 us
    another operation x1, loops' own time, local(): return lax.map(single, jnp.arange(local_count, dtype=jnp.int32))  21.8 us
    cos x16, other arithmetic, rope_table(): return (jnp.cos(angles), jnp.sin(angles))  13.1 us
    scatter x8, other arithmetic, attend(): key_rows = key_rows.at[places].set(fresh_keys[:recomputed])  12.2 us
    another operation x16, other arithmetic  11.6 us
    while x4, local copies, waits for them, and re-layouts, local(): return lax.map(single, jnp.arange(local_count, dtype=jnp.int32))  11 us
  transfers between devices with their start and end apart: 3, of which 3 were waited for; matrix products, arithmetic and copies ran while one was open for 0% of the time, Pallas kernels for 0%

commit v1 on v0

v1 whole, which is shorter than its diff:
```python
import functools
import math

import jax
import jax.numpy as jnp
from jax import lax
from jax.experimental import pallas as pl
from jax.experimental.pallas import tpu as pltpu
from jax.sharding import PartitionSpec as P

KV_HEADS = 8
LOG2E = 1.4426950408889634
BIG = 2.0**100
MIB = 1 << 20
SINE = (6.283185272447939, -41.34169703819957, 81.60502363802357, -76.7015376701132,
        42.01607576102491, -14.868322748754837, 3.1993388405088488)


def shifted(value, axis, by):
    devices = lax.axis_size(axis)
    return lax.ppermute(value, axis, [(i, (i + by) % devices) for i in range(devices)])


def sine_of_turns(t):
    r = t - jnp.floor(t + 0.5)
    square = r * r
    value = jnp.full(r.shape, SINE[-1], jnp.float32)
    for coefficient in SINE[-2::-1]:
        value = value * square + coefficient
    return value * r


def turns_per_step(index, dim):
    return jnp.exp(-(2.0 / dim) * math.log(500000.0) * index.astype(jnp.float32)) * (0.5 / math.pi)


def turn(rows, cosines, sines):
    return rows * cosines + pltpu.roll(rows, rows.shape[-1] // 2, 1) * sines


class Plan:
    def __init__(self, span_kv, request_spans, recomp_pos, new_q, groups):
        self.groups = groups
        self.per_group, self.length, width = span_kv.shape
        self.dim = width // 2
        self.piece = 2 * self.dim
        self.join = request_spans.shape[1]
        self.fresh = recomp_pos.shape[2]
        self.requests, self.rows, query_width = new_q.shape
        self.heads = query_width // self.dim
        self.recomputed = self.join * self.fresh
        self.decode = self.rows - self.recomputed
        self.block = self.heads * self.fresh
        self.tail = self.heads * self.decode
        self.height = self.join * self.block + self.tail
        self.slots = groups * self.per_group


def pack_kernel(plan, spans, *outs):
    dim, piece = plan.dim, plan.piece
    for s in range(plan.per_group):
        for first in range(0, plan.length, piece):
            keys = spans[s, first : first + piece, :dim].astype(jnp.float32)
            outs[s][first : first + dim, :] = keys.T.astype(jnp.bfloat16)
            outs[s][first + dim : first + piece, :dim] = spans[s, first : first + dim, dim:]
            outs[s][first + dim : first + piece, dim:] = spans[s, first + dim : first + piece, dim:]


def plan_work(plan, me, home, spans, work):
    stride = plan.requests + 1
    for chunk in range(plan.slots):
        for i in range(stride):
            work[chunk * stride + i] = 0
    for u in range(plan.requests):
        for j in range(plan.join):
            slot = home[spans[j, me[0] * plan.requests + u]]
            group = lax.div(slot, plan.per_group)
            distance = lax.rem(group - me[0] + plan.groups, plan.groups)
            chunk = distance * plan.per_group + slot - group * plan.per_group
            count = work[chunk * stride] + 1
            work[chunk * stride] = count
            work[chunk * stride + count] = u * plan.join + j
            work[plan.slots * stride + u * plan.join + j] = chunk


def prepare_kernel(plan, me, home, spans, newq_hbm, newkv_hbm, recomp, q_out, acc, places, turns, marks, fresh_k, fresh_v,
                   last_kv, work, tok, newq, newkv, table, flat, tails, column, mask, sems):
    loads = [pltpu.make_async_copy(newq_hbm, newq, sems.at[0]), pltpu.make_async_copy(newkv_hbm, newkv, sems.at[1])]
    for load in loads:
        load.start()
    plan_work(plan, me, home, spans, work)
    dim, fresh, requests, heads, block = plan.dim, plan.fresh, plan.requests, plan.heads, plan.block
    recomputed, decode, join = plan.recomputed, plan.decode, plan.join
    half = dim // 2
    scale = LOG2E / (dim**0.5)
    tok[...] = jnp.zeros(tok.shape, jnp.float32)

    row = lax.broadcasted_iota(jnp.int32, (dim, dim), 0)
    rate = turns_per_step(lax.rem(row, half), dim)
    phase = jnp.where(row < half, 0.25, 0.0)
    for j in range(join):
        turns[j] = sine_of_turns(rate * float(j * plan.length) + phase)

    row = lax.broadcasted_iota(jnp.int32, (plan.height, dim), 0)
    lane = lax.broadcasted_iota(jnp.int32, (plan.height, dim), 1)
    counts = ((lane >= fresh) & (lane < 2 * fresh)) | ((row < block) & (lane == lax.rem(row, fresh)))
    marks[...] = jnp.where(counts, 1.0, 0.0).astype(jnp.bfloat16)

    row = lax.broadcasted_iota(jnp.int32, (plan.height, recomputed), 0)
    key = lax.broadcasted_iota(jnp.int32, (plan.height, recomputed), 1)
    reach = (row // block) * fresh + lax.rem(row, fresh)
    mask[...] = jnp.where((row >= join * block) | (key <= reach), 0.0, -BIG)

    lane = lax.broadcasted_iota(jnp.int32, (fresh, dim), 1)
    rate = turns_per_step(lax.rem(lane, half), dim)
    signed = jnp.where(lane < half, -rate, rate)

    def places_of(u, carry):
        request = me[0] * requests + u
        column[:join, :fresh] = recomp[request].astype(jnp.float32)
        upright = column[...].T
        for j in range(join):
            inside = jnp.broadcast_to(upright[:fresh, j : j + 1], (fresh, dim))
            places[u * join + j] = inside
            at = inside + float(j * plan.length)
            table[0, u, j * fresh : (j + 1) * fresh, :] = sine_of_turns(at * rate + 0.25)
            table[1, u, j * fresh : (j + 1) * fresh, :] = sine_of_turns(at * signed)
        return carry

    column[...] = jnp.zeros(column.shape, jnp.float32)
    lax.fori_loop(0, requests, places_of, 0)
    step = lax.broadcasted_iota(jnp.int32, (decode * requests, dim), 0) // requests
    at = (join * plan.length + step).astype(jnp.float32)
    lane = lax.broadcasted_iota(jnp.int32, (decode * requests, dim), 1)
    rate = turns_per_step(lax.rem(lane, half), dim)
    last_cos = sine_of_turns(at * rate + 0.25)
    last_sin = sine_of_turns(at * jnp.where(lane < half, -rate, rate))

    for load in loads:
        load.wait()

    def queries_of(j, carry):
        rows = pl.ds(pl.multiple_of(j * fresh, fresh), fresh)
        for head in range(heads):
            x = newq[rows, :, head * dim : (head + 1) * dim].astype(jnp.float32)
            flat[head, : fresh * requests, :] = x.reshape(fresh * requests, dim)
        for u in range(requests):
            cosines = table[0, u, rows, :] * scale
            sines = table[1, u, rows, :] * scale
            for head in range(heads):
                y = turn(flat[head, pl.ds(u, fresh, stride=requests), :], cosines, sines)
                q_out[u, pl.ds(pl.multiple_of(j * block + head * fresh, fresh), fresh), :] = y.astype(jnp.bfloat16)
        return carry

    lax.fori_loop(0, join, queries_of, 0)
    for head in range(heads):
        x = newq[recomputed:, :, head * dim : (head + 1) * dim].astype(jnp.float32)
        y = turn(x.reshape(decode * requests, dim), last_cos, last_sin) * scale
        tails[head * decode * requests : (head + 1) * decode * requests, :] = y
    for u in range(requests):
        y = tails[pl.ds(u, plan.tail, stride=requests), :]
        q_out[u, join * block :, :] = y.astype(jnp.bfloat16)

    x = newkv[:recomputed, :, :].astype(jnp.float32)
    for side in range(2):
        flat[side] = x[:, :, side * dim : (side + 1) * dim].reshape(recomputed * requests, dim)
    x = newkv[recomputed:, :, :].astype(jnp.float32)
    last_kv[:, :dim] = turn(x[:, :, :dim].reshape(decode * requests, dim), last_cos, last_sin).astype(
        jnp.bfloat16
    ).astype(jnp.float32)
    last_kv[:, dim:] = x[:, :, dim:].reshape(decode * requests, dim)
    ones = jnp.ones((recomputed, dim), jnp.bfloat16)
    which = lax.rem(lax.broadcasted_iota(jnp.int32, (plan.tail, dim), 0), decode)

    def fresh_of(u, carry):
        y = turn(flat[0, pl.ds(u, recomputed, stride=requests), :], table[0, u], table[1, u])
        fresh_k[u] = y.T.astype(jnp.bfloat16)
        fresh_v[u] = flat[1, pl.ds(u, recomputed, stride=requests), :].astype(jnp.bfloat16)
        s = jnp.dot(q_out[u], fresh_k[u], preferred_element_type=jnp.float32)
        p = jnp.exp2(s + mask[...]).astype(jnp.bfloat16)
        values = jnp.concatenate([fresh_v[u], ones], 1)
        acc[u] = jnp.dot(p, values, preferred_element_type=jnp.float32)
        mine = q_out[u, join * block :, :].astype(jnp.float32)
        for d in range(decode):
            pair = last_kv[pl.ds(d * requests + u, 1), :]
            s = jnp.sum(mine * pair[:, :dim], 1, keepdims=True)
            p = jnp.where(which >= d, jnp.exp2(jnp.broadcast_to(s, which.shape)), 0.0)
            p = p.astype(jnp.bfloat16).astype(jnp.float32)
            acc[u, join * block :, :dim] += p * pair[:, dim:]
            acc[u, join * block :, dim:] += p
        return carry

    lax.fori_loop(0, requests, fresh_of, 0)


def spread_chunk(plan, chunk, values):
    dim, piece = plan.dim, plan.piece
    for first in range(0, chunk.shape[0], piece):
        values[first : first + dim, :dim] = chunk[first + dim : first + piece, :dim]
        values[first + dim : first + piece, :dim] = chunk[first + dim : first + piece, dim:]


def shift_keys(plan, chunk, first_token, place, angles, keys):
    dim, piece, fresh = plan.dim, plan.piece, plan.fresh
    half = dim // 2
    wide = lambda x: jnp.concatenate([x] * (piece // dim), 1)
    cosines, sines = wide(angles[:half]), wide(angles[half:])
    place = wide(place)
    for first in range(0, chunk.shape[0], piece):
        columns = slice(first, first + piece)
        a = chunk[first : first + half, :].astype(jnp.float32)
        b = chunk[first + half : first + dim, :].astype(jnp.float32)
        keys[:half, columns] = (a * cosines - b * sines).astype(jnp.bfloat16)
        keys[half:dim, columns] = (b * cosines + a * sines).astype(jnp.bfloat16)
        token = lax.broadcasted_iota(jnp.int32, (fresh, piece), 1) + (first_token + first)
        token = token.astype(jnp.float32)
        keys[dim : dim + fresh, columns] = jnp.where(token > place, -BIG, 0.0).astype(jnp.bfloat16)
        keys[dim + fresh : dim + 2 * fresh, columns] = jnp.where(token == place, -BIG, 0.0).astype(jnp.bfloat16)


def chunk_kernel(plan, order, work, chunk, places, turns, marks, q, _, acc, tok, keys, values):
    dim, block, join = plan.dim, plan.block, plan.join
    tok[...] = jnp.zeros(tok.shape, jnp.float32)
    length = chunk.shape[0]
    keys[dim + 2 * plan.fresh :, :] = jnp.zeros((dim - 2 * plan.fresh, length), jnp.bfloat16)
    values[:, dim:] = jnp.ones((length, dim), jnp.bfloat16)
    spread_chunk(plan, chunk, values)
    base = order * (plan.requests + 1)

    def prepare(n):
        place = work[base + 1 + n]
        shift_keys(plan, chunk, 0, places[place], turns[lax.rem(place, join)], keys)

    def one(n, carry):
        place = work[base + 1 + n]
        u = lax.div(place, join)
        j = place - u * join
        for k in range(join):

            @pl.when(j == k)
            def _():
                count = plan.height - k * block
                left = jnp.concatenate([q[u, k * block :, :], marks[:count, :]], 1)
                s = jnp.dot(left, keys[...], preferred_element_type=jnp.float32)
                prepare(jnp.minimum(n + 1, plan.requests - 1))
                p = jnp.exp2(s).astype(jnp.bfloat16)
                acc[u, k * block :, :] += jnp.dot(p, values[...], preferred_element_type=jnp.float32)

        return carry

    prepare(0)
    lax.fori_loop(0, work[base], one, 0)


def finish_kernel(plan, work, *refs):
    chunks = refs[: plan.slots]
    (places, turns, marks, q, acc, fresh_k, fresh_v, last_kv, out,
     done, flat, tails, joined, keys, values, top, total, peak, sems, load) = refs[plan.slots :]
    dim, fresh, requests, heads, block = plan.dim, plan.fresh, plan.requests, plan.heads, plan.block
    recomputed, decode, join = plan.recomputed, plan.decode, plan.join

    def put(u, source, seen):
        least, most, odd = seen
        for head in range(heads):
            rows = slice(head * fresh, (head + 1) * fresh)
            a, weight = source(rows)
            o = a / weight
            least, most = jnp.minimum(least, weight), jnp.maximum(most, weight)
            odd = odd + o * 0.0
            flat[head, pl.ds(u, fresh, stride=requests), :] = o
        return least, most, odd

    def put_tail(u, a, weight):
        o = a / weight
        tails[pl.ds(u, plan.tail, stride=requests), :] = o
        return weight, weight, o * 0.0

    def write(j):
        rows = pl.ds(j * fresh, fresh)
        for head in range(heads):
            x = flat[head].reshape(fresh, requests, dim)
            done[rows, :, head * dim : (head + 1) * dim] = x.astype(jnp.bfloat16)
        return rows

    def write_tail():
        for head in range(heads):
            x = tails[head * decode * requests : (head + 1) * decode * requests, :]
            done[recomputed:, :, head * dim : (head + 1) * dim] = x.reshape(decode, requests, dim).astype(jnp.bfloat16)

    def send(j):
        rows = pl.ds(j * fresh, fresh) if j < join else pl.ds(recomputed, decode)
        return pltpu.make_async_copy(done.at[rows], out.at[rows], sems.at[j])

    shape = (fresh, dim)
    seen = (jnp.full(shape, 1.0, jnp.float32), jnp.full(shape, 1.0, jnp.float32), jnp.zeros(shape, jnp.float32))
    tail_good = jnp.bool_(True)
    for u in range(requests):
        a = acc[u, join * block :, :]
        least, most, odd = put_tail(u, a[:, :dim], a[:, dim:])
        tail_good &= (jnp.min(least) > 2.0**-60) & (jnp.max(most) < 2.0**60) & (jnp.min(odd) == 0.0)
    write_tail()
    send(join).start()
    for j in range(join):
        for u in range(requests):
            source = lambda rows: (
                acc[u, j * block + rows.start : j * block + rows.stop, :dim],
                acc[u, j * block + rows.start : j * block + rows.stop, dim:],
            )
            seen = put(u, source, seen)
        write(j)
        send(j).start()
    least, most, odd = seen
    good = tail_good & (jnp.min(least) > 2.0**-60) & (jnp.max(most) < 2.0**60) & (jnp.min(odd) == 0.0)
    for j in range(join + 1):
        send(j).wait()

    @pl.when(jnp.logical_not(good))
    def _():
        keys[dim + 2 * fresh :, :] = jnp.zeros((dim - 2 * fresh, plan.length), jnp.bfloat16)
        unseen = (jnp.full(shape, 1.0, jnp.float32), jnp.full(shape, 1.0, jnp.float32), jnp.zeros(shape, jnp.float32))

        def fold(rows, s, v):
            before = peak[rows, :]
            now = jnp.maximum(before, jnp.max(s, 1, keepdims=True))
            peak[rows, :] = now
            fade = jnp.exp2(before - now)
            p = jnp.exp2(s - now[:, :1]).astype(jnp.bfloat16)
            total[rows, :] = total[rows, :] * fade + jnp.sum(p.astype(jnp.float32), 1, keepdims=True)
            top[rows, :] = top[rows, :] * fade + jnp.dot(p, v, preferred_element_type=jnp.float32)

        def sums(u, j):
            count = block if j < join else plan.tail
            every = pl.ds(0, count)
            peak[every, :] = jnp.full((count, dim), -3.0e38, jnp.float32)
            top[every, :] = jnp.zeros((count, dim), jnp.float32)
            total[every, :] = jnp.zeros((count, dim), jnp.float32)
            mine = q[u, j * block : j * block + count, :]
            s = jnp.dot(mine, fresh_k[u], preferred_element_type=jnp.float32)
            key = lax.broadcasted_iota(jnp.int32, s.shape, 1)
            row = lax.broadcasted_iota(jnp.int32, s.shape, 0)
            if j < join:
                s = jnp.where(key <= j * fresh + lax.rem(row, fresh), s, -BIG)
            fold(every, s, fresh_v[u])
            for k in range(min(j + 1, join)):
                for order, chunk in enumerate(chunks):

                    @pl.when(work[plan.slots * (requests + 1) + u * join + k] == order)
                    def _():
                        copy = pltpu.make_async_copy(chunk, joined, load.at[0])
                        copy.start()
                        copy.wait()

                spread_chunk(plan, joined, values)
                shift_keys(plan, joined, 0, places[u * join + k], turns[k], keys)
                mark = marks[:count, :] if k == j else marks[block : block + count, :]
                left = jnp.concatenate([mine, mark], 1)
                s = jnp.dot(left, keys[...], preferred_element_type=jnp.float32)
                fold(every, s, values[:, :dim])
            if j == join:
                which = lax.rem(lax.broadcasted_iota(jnp.int32, (count, dim), 0), decode)
                for d in range(decode):
                    pair = last_kv[pl.ds(d * requests + u, 1), :]
                    s = jnp.sum(mine.astype(jnp.float32) * pair[:, :dim], 1, keepdims=True)
                    s = jnp.where(which >= d, s, -BIG)
                    before = peak[every, :]
                    now = jnp.maximum(before, s)
                    peak[every, :] = now
                    p = jnp.exp2(s - now)
                    total[every, :] = total[every, :] * jnp.exp2(before - now) + p
                    top[every, :] = top[every, :] * jnp.exp2(before - now) + p * pair[:, dim:]

        for j in range(join + 1):

            def again(u, carry):
                sums(u, j)
                if j < join:
                    put(u, lambda rows: (top[rows, :], total[rows, :]), unseen)
                else:
                    put_tail(u, top[: plan.tail, :], total[: plan.tail, :])
                return carry

            lax.fori_loop(0, requests, again, 0)
            if j < join:
                write(j)
            else:
                write_tail()
            copy = send(j)
            copy.start()
            copy.wait()


def local(span_kv, span_home, request_spans, recomp_pos, new_q, new_kv):
    groups = lax.axis_size("store") // KV_HEADS
    me = (lax.axis_index("store") // KV_HEADS).reshape(1).astype(jnp.int32)
    plan = Plan(span_kv, request_spans, recomp_pos, new_q, groups)
    dim, join, requests = plan.dim, plan.join, plan.requests
    vmem = pl.BlockSpec(memory_space=pltpu.VMEM)
    smem = pl.BlockSpec(memory_space=pltpu.SMEM)
    anywhere = pl.BlockSpec(memory_space=pl.ANY)
    params = lambda mib: pltpu.CompilerParams(vmem_limit_bytes=mib * MIB)
    inside = lambda x: pltpu.with_memory_space_constraint(x, pltpu.VMEM)
    outside = lambda x: pltpu.with_memory_space_constraint(x, pltpu.HBM)
    cost = lambda us: pl.CostEstimate(flops=int(us * 1.1e9), bytes_accessed=0, transcendentals=0)

    packed = pl.pallas_call(
        functools.partial(pack_kernel, plan),
        out_shape=[pltpu.VMEM((plan.length, 2 * dim), jnp.bfloat16)] * plan.per_group,
        in_specs=[vmem],
        out_specs=[vmem] * plan.per_group,
        compiler_params=params(6),
        cost_estimate=cost(1.0),
        name="pack",
    )(span_kv)

    moving = [shifted(x, "store", -KV_HEADS) for x in packed] if groups > 1 else []

    spans = request_spans.T

    token = pltpu.VMEM((8, 128), jnp.float32)
    acc_type = pltpu.VMEM((requests, plan.height, 2 * dim), jnp.float32)
    q, acc, places, turns, marks, fresh_k, fresh_v, last_kv, work, tok = pl.pallas_call(
        functools.partial(prepare_kernel, plan),
        out_shape=[
            pltpu.VMEM((requests, plan.height, dim), jnp.bfloat16),
            acc_type,
            pltpu.VMEM((requests * join, plan.fresh, dim), jnp.float32),
            pltpu.VMEM((join, dim, dim), jnp.float32),
            pltpu.VMEM((plan.height, dim), jnp.bfloat16),
            pltpu.VMEM((requests, dim, plan.recomputed), jnp.bfloat16),
            pltpu.VMEM((requests, plan.recomputed, dim), jnp.bfloat16),
            pltpu.VMEM((plan.decode * requests, 2 * dim), jnp.float32),
            pltpu.SMEM((plan.slots * (requests + 1) + requests * join,), jnp.int32),
            token,
        ],
        in_specs=[smem] * 3 + [anywhere] * 2 + [vmem],
        out_specs=[vmem] * 8 + [smem, vmem],
        scratch_shapes=[
            pltpu.VMEM((plan.rows, requests, new_q.shape[2]), jnp.bfloat16),
            pltpu.VMEM((plan.rows, requests, 2 * dim), jnp.bfloat16),
            pltpu.VMEM((2, requests, plan.recomputed, dim), jnp.float32),
            pltpu.VMEM((plan.heads, plan.recomputed * requests, dim), jnp.float32),
            pltpu.VMEM((plan.heads * plan.decode * requests, dim), jnp.float32),
            pltpu.VMEM((dim, dim), jnp.float32),
            pltpu.VMEM((plan.height, plan.recomputed), jnp.float32),
            pltpu.SemaphoreType.DMA((2,)),
        ],
        compiler_params=params(20),
        cost_estimate=cost(6.0),
        name="prepare",
    )(me, span_home, spans, outside(new_q.transpose(1, 0, 2)), outside(new_kv.transpose(1, 0, 2)), recomp_pos)
    work = pltpu.with_memory_space_constraint(work, pltpu.SMEM)

    def take(order, chunk, acc):
        return pl.pallas_call(
            functools.partial(chunk_kernel, plan, order),
            out_shape=[acc_type, token],
            in_specs=[smem] + [vmem] * 6,
            out_specs=[vmem] * 2,
            input_output_aliases={6: 0},
            scratch_shapes=[
                pltpu.VMEM((2 * dim, plan.length), jnp.bfloat16),
                pltpu.VMEM((plan.length, 2 * dim), jnp.bfloat16),
            ],
            compiler_params=params(12),
            cost_estimate=cost(2.5),
            name="chunk",
        )(work, *map(inside, [chunk, places, turns, marks, q, acc]))

    def onward(k, tok):
        if k + plan.per_group < plan.slots - plan.per_group:
            held, tok = lax.optimization_barrier((buffers[plan.per_group + k], tok))
            buffers.append(shifted(held, "store", -KV_HEADS))

    buffers = list(packed) + moving
    onward(0, tok)
    for order in range(plan.slots):
        acc, tok = take(order, buffers[order], acc)
        if order < plan.per_group - 1:
            onward(order + 1, tok)
        elif order >= plan.per_group:
            onward(order, tok)

    out = pl.pallas_call(
        functools.partial(finish_kernel, plan),
        out_shape=jax.ShapeDtypeStruct((plan.rows, requests, new_q.shape[2]), jnp.bfloat16),
        in_specs=[smem] + [anywhere] * len(buffers) + [vmem] * 8,
        out_specs=anywhere,
        scratch_shapes=[
            pltpu.VMEM((plan.rows, requests, new_q.shape[2]), jnp.bfloat16),
            pltpu.VMEM((plan.heads, plan.fresh * requests, dim), jnp.float32),
            pltpu.VMEM((plan.heads * plan.decode * requests, dim), jnp.float32),
            pltpu.VMEM((plan.length, 2 * dim), jnp.bfloat16),
            pltpu.VMEM((2 * dim, plan.length), jnp.bfloat16),
            pltpu.VMEM((plan.length, 2 * dim), jnp.bfloat16),
            pltpu.VMEM((plan.block, dim), jnp.float32),
            pltpu.VMEM((plan.block, dim), jnp.float32),
            pltpu.VMEM((plan.block, dim), jnp.float32),
            pltpu.SemaphoreType.DMA((join + 1,)),
            pltpu.SemaphoreType.DMA((1,)),
        ],
        compiler_params=params(24),
        cost_estimate=cost(3.0),
        name="finish",
    )(work, *buffers, *map(inside, [places, turns, marks, q, acc, fresh_k, fresh_v, last_kv]))
    return out.transpose(1, 0, 2)


def solution(mesh):
    return jax.shard_map(
        local,
        mesh=mesh,
        in_specs=(
            P(("groups", "store"), None, None),
            P("groups"),
            P("groups", None),
            P("groups", None, None),
            P(("groups", "store"), None, None),
            P(("groups", "store"), None, None),
        ),
        out_specs=P(("groups", "store"), None, None),
        check_vma=False,
    )
```

time: 320 us -> 157 us (0.49); the launches traced: 318 us -> 160 us
  Pallas kernels: 0 us -> 134 us
  matrix products: 114 us -> 0 us
  other arithmetic: 66.2 us -> 0 us
  local copies, waits for them, and re-layouts: 69.4 us -> 3.22 us
  waiting for transfers between devices: 42.8 us -> 1.73 us
  loops' own time: 22 us -> 0 us
  starting transfers between devices: 3.19 us -> 21 us
    pallas_call x0 -> x11, Pallas kernels: none -> 134 us  [the longest x1 96 us: local(): pl.pallas_call(functools.partial(finish_kernel, plan), out_shape=jax.Shap...]
    sub x8 -> x0, matrix products: 73.1 us -> none  [attend(): powers = jnp.where(visible, jnp.exp(scores - peaks), jnp.float32(0.0))]
    dot_general x8 -> x0, matrix products: 41.1 us -> none  [attend(): jnp.einsum('hrk,kd->rhd', weights, value_rows, preferred_element_type=jnp...]
    ppermute x3 -> x6, waiting for transfers between devices: 42.8 us -> 1.73 us  [shifted(): lax.ppermute(value, axis, [(i, (i + by) % devices) for i in range(devices)])]
    another operation x2 -> x0, loops' own time: 22 us -> none  [the longest x1 21.8 us: local(): return lax.map(single, jnp.arange(local_count, dtype=jnp.int32))]
    ppermute x3 -> x6, starting transfers between devices: 3.19 us -> 21 us  [shifted(): lax.ppermute(value, axis, [(i, (i + by) % devices) for i in range(devices)])]
    cos x16 -> x0, other arithmetic: 13.1 us -> none  [rope_table(): return (jnp.cos(angles), jnp.sin(angles))]
    scatter x8 -> x0, other arithmetic: 12.2 us -> none  [attend(): key_rows = key_rows.at[places].set(fresh_keys[:recomputed])]
  transfers between devices with their start and end apart: 3 -> 6, of which waited for: 3 -> 2; matrix products, arithmetic and copies ran while one was open for 0% -> 0% of each run, Pallas kernels for 0% -> 19%
where the time goes in v1:
time: 157 us; the launch traced here: 160 us
  Pallas kernels  134 us (85%)
  starting transfers between devices  21 us (13%)
  local copies, waits for them, and re-layouts  3.22 us (2%)
  waiting for transfers between devices  1.73 us (1%)
    pallas_call x1, Pallas kernels, local(): pl.pallas_call(functools.partial(finish_kernel, plan), out_shape=jax.Shap...  96 us
    pallas_call x8, Pallas kernels, take(): pl.pallas_call(functools.partial(chunk_kernel, plan, order), out_shape=[a...  27.2 us
    ppermute x6, starting transfers between devices, shifted(): lax.ppermute(value, axis, [(i, (i + by) % devices) for i in range(devices)])  21 us
    pallas_call x1, Pallas kernels, local(): pl.pallas_call(functools.partial(prepare_kernel, plan), out_shape=[pltpu....  10.5 us
    unnamed x8, local copies, waits for them, and re-layouts  3.22 us
  transfers between devices with their start and end apart: 6, of which 2 were waited for; matrix products, arithmetic and copies ran while one was open for 0% of the time, Pallas kernels for 19%

profile of v1, /device:TPU:0, one launch (start us, length us, event | category | flops | bytes accessed | tf_op | source)
XLA Modules:
  0.0 160.0 jit_solution(7315174981891492422)
XLA Ops:
  0.0 0.0 copy-start
  0.0 1.0 copy-done
  1.0 0.1 pack.1
  1.2 5.1 %collective-permute-start = (bf16[512,256]{1,0:T(8,128)(2,1)S(1)}, bf16[512,256]{1,0:T(8,128)(2,1)S(1)}, u32[]{:S(2)}, u32[]{:S(2)}) collective-permute-start(bf16[512,256]{1,0:T(8,128)(2,1)S(1)} %get-tuple-element.25.chunk.refs_0_), channel_id=1, source_target_pairs={{0,24},{1,25},{2,26},{3,27},{4,28},{5,29},{6,30},{7,31},{8,0},{9,1... | collective-permute-start | bytes 786440 | tf_op jit(solution)/shard_map/ppermute | solution.py:21
  6.3 0.4 collective-permute-start.1
  6.7 0.0 copy-start.1
  6.7 0.8 copy-done.1
  7.6 0.0 copy-start.2
  7.6 0.7 copy-done.2
  8.3 0.0 copy-start.3
  8.3 0.7 copy-done.3
  8.9 10.5 %prepare.1 = (bf16[8,1040,128]{2,1,0:T(8,128)(2,1)S(1)}, f32[8,1040,256]{2,1,0:T(8,128)S(1)}, f32[32,32,128]{2,1,0:T(8,128)S(1)}, f32[4,128,128]{2,1,0:T(8,128)S...) custom-call(s32[1]{0:T(128)} %bitcast.me, ...), custom_call_target="tpu_custom_call" | custom-call | flops 6600000000 | tf_op jit(solution)/shard_map/prepare/pallas_call | solution.py:421
  19.4 1.7 %chunk.8 = (f32[8,1040,256]{2,1,0:T(8,128)S(1)}, f32[8,128]{1,0:T(8,128)}) custom-call(s32[104]{0:T(128)S(4)} %get-tuple-element.24.work, bf16[512,256]{1,0:T(8,128)(2,1)S(1)} %get-tuple-element.25.chunk.refs_0_, f32[32,32,128]{2,1,0:T(8,128)S(1)} %get-tuple-element.27.places.refs_8_, ...), custom_call_target="tpu_custom_call", output_to_operand_aliasing={{0}: (6, {})} | custom-call | flops 2750000128 | tf_op jit(solution)/shard_map/chunk/pallas_call | solution.py:454
  21.2 2.3 %chunk.9 = (f32[8,1040,256]{2,1,0:T(8,128)S(1)}, f32[8,128]{1,0:T(8,128)}) custom-call(s32[104]{0:T(128)S(4)} %get-tuple-element.24.work, bf16[512,256]{1,0:T(8,128)(2,1)S(1)} %get-tuple-element.26.chunk.refs_1_, f32[32,32,128]{2,1,0:T(8,128)S(1)} %get-tuple-element.27.places.refs_8_, ...), custom_call_target="tpu_custom_call", output_to_operand_aliasing={{0}: (6, {})} | custom-call | flops 2750000128 | tf_op jit(solution)/shard_map/chunk/pallas_call | solution.py:454
  23.4 0.0 collective-permute-done.chunk.refs_2_
  23.4 6.8 %collective-permute-start.2 = (bf16[512,256]{1,0:T(8,128)(2,1)S(1)}, bf16[512,256]{1,0:T(8,128)(2,1)S(1)}, u32[]{:S(2)}, u32[]{:S(2)}) collective-permute-start(bf16[512,256]{1,0:T(8,128)(2,1)S(1)} %collective-permute-done.chunk.refs_2_), channel_id=1, source_target_pairs={{0,24},{1,25},{2,26},{3,27},{4,28},{5,29},{6,30},{7,31},{8,0},{9,1... | collective-permute-start | bytes 786440 | tf_op jit(solution)/shard_map/ppermute | solution.py:21
  30.2 0.0 collective-permute-done.1.chunk.refs_3_
  30.2 0.1 collective-permute-start.3
  30.3 3.5 %chunk.10 = (f32[8,1040,256]{2,1,0:T(8,128)S(1)}, f32[8,128]{1,0:T(8,128)}) custom-call(s32[104]{0:T(128)S(4)} %get-tuple-element.24.work, bf16[512,256]{1,0:T(8,128)(2,1)S(1)} %collective-permute-done.chunk.refs_2_, f32[32,32,128]{2,1,0:T(8,128)S(1)} %get-tuple-element.27.places.refs_8_, ...), custom_call_target="tpu_custom_call", output_to_operand_aliasing={{0}: (6, {})} | custom-call | flops 2750000128 | tf_op jit(solution)/shard_map/chunk/pallas_call | solution.py:454
  33.8 2.8 %chunk.11 = (f32[8,1040,256]{2,1,0:T(8,128)S(1)}, f32[8,128]{1,0:T(8,128)}) custom-call(s32[104]{0:T(128)S(4)} %get-tuple-element.24.work, bf16[512,256]{1,0:T(8,128)(2,1)S(1)} %collective-permute-done.1.chunk.refs_3_, f32[32,32,128]{2,1,0:T(8,128)S(1)} %get-tuple-element.27.places.refs_8_, ...), custom_call_target="tpu_custom_call", output_to_operand_aliasing={{0}: (6, {})} | custom-call | flops 2750000128 | tf_op jit(solution)/shard_map/chunk/pallas_call | solution.py:454
  36.6 0.4 collective-permute-done.2.chunk.refs_4_
  37.0 4.3 %collective-permute-start.4 = (bf16[512,256]{1,0:T(8,128)(2,1)S(1)}, bf16[512,256]{1,0:T(8,128)(2,1)S(1)}, u32[]{:S(2)}, u32[]{:S(2)}) collective-permute-start(bf16[512,256]{1,0:T(8,128)(2,1)S(1)} %collective-permute-done.2.chunk.refs_4_), channel_id=1, source_target_pairs={{0,24},{1,25},{2,26},{3,27},{4,28},{5,29},{6,30},{7,31},{8,0},{9,1... | collective-permute-start | bytes 786440 | tf_op jit(solution)/shard_map/ppermute | solution.py:21
  41.3 1.3 collective-permute-done.3.chunk.refs_5_
  42.6 4.3 %collective-permute-start.5 = (bf16[512,256]{1,0:T(8,128)(2,1)S(1)}, bf16[512,256]{1,0:T(8,128)(2,1)S(1)}, u32[]{:S(2)}, u32[]{:S(2)}) collective-permute-start(bf16[512,256]{1,0:T(8,128)(2,1)S(1)} %collective-permute-done.3.chunk.refs_5_), channel_id=1, source_target_pairs={{0,24},{1,25},{2,26},{3,27},{4,28},{5,29},{6,30},{7,31},{8,0},{9,1... | collective-permute-start | bytes 786440 | tf_op jit(solution)/shard_map/ppermute | solution.py:21
  46.9 4.1 %chunk.12 = (f32[8,1040,256]{2,1,0:T(8,128)S(1)}, f32[8,128]{1,0:T(8,128)}) custom-call(s32[104]{0:T(128)S(4)} %get-tuple-element.24.work, bf16[512,256]{1,0:T(8,128)(2,1)S(1)} %collective-permute-done.2.chunk.refs_4_, f32[32,32,128]{2,1,0:T(8,128)S(1)} %get-tuple-element.27.places.refs_8_, ...), custom_call_target="tpu_custom_call", output_to_operand_aliasing={{0}: (6, {})} | custom-call | flops 2750000128 | tf_op jit(solution)/shard_map/chunk/pallas_call | solution.py:454
  51.0 2.1 %chunk.13 = (f32[8,1040,256]{2,1,0:T(8,128)S(1)}, f32[8,128]{1,0:T(8,128)}) custom-call(s32[104]{0:T(128)S(4)} %get-tuple-element.24.work, bf16[512,256]{1,0:T(8,128)(2,1)S(1)} %collective-permute-done.3.chunk.refs_5_, f32[32,32,128]{2,1,0:T(8,128)S(1)} %get-tuple-element.27.places.refs_8_, ...), custom_call_target="tpu_custom_call", output_to_operand_aliasing={{0}: (6, {})} | custom-call | flops 2750000128 | tf_op jit(solution)/shard_map/chunk/pallas_call | solution.py:454
  53.0 0.0 collective-permute-done.4.chunk.refs_6_
  53.0 3.4 %chunk.14 = (f32[8,1040,256]{2,1,0:T(8,128)S(1)}, f32[8,128]{1,0:T(8,128)}) custom-call(s32[104]{0:T(128)S(4)} %get-tuple-element.24.work, bf16[512,256]{1,0:T(8,128)(2,1)S(1)} %collective-permute-done.4.chunk.refs_6_, f32[32,32,128]{2,1,0:T(8,128)S(1)} %get-tuple-element.27.places.refs_8_, ...), custom_call_target="tpu_custom_call", output_to_operand_aliasing={{0}: (6, {})} | custom-call | flops 2750000128 | tf_op jit(solution)/shard_map/chunk/pallas_call | solution.py:454
  56.4 0.0 collective-permute-done.5.chunk.refs_7_
  56.4 7.4 %chunk.15 = (f32[8,1040,256]{2,1,0:T(8,128)S(1)}, f32[8,128]{1,0:T(8,128)}) custom-call(s32[104]{0:T(128)S(4)} %get-tuple-element.24.work, bf16[512,256]{1,0:T(8,128)(2,1)S(1)} %collective-permute-done.5.chunk.refs_7_, f32[32,32,128]{2,1,0:T(8,128)S(1)} %get-tuple-element.27.places.refs_8_, ...), custom_call_target="tpu_custom_call", output_to_operand_aliasing={{0}: (6, {})} | custom-call | flops 2750000128 | tf_op jit(solution)/shard_map/chunk/pallas_call | solution.py:454
  63.8 96.0 %finish.1 = bf16[130,8,1024]{2,1,0:T(8,128)(2,1)} custom-call(s32[104]{0:T(128)S(4)} %get-tuple-element.24.work, bf16[512,256]{1,0:T(8,128)(2,1)S(1)} %get-tuple-element.25.chunk.refs_0_, bf16[512,256]{1,0:T(8,128)(2,1)S(1)} %get-tuple-element.26.chunk.refs_1_, bf16[512,256]{1,0:T(8,128)(2,1)S(1)} %collective-permute-done.chunk.refs_2_, ...), custom_call_target="tpu_custom_call" | custom-call | flops 3300000000 | tf_op jit(solution)/shard_map/finish/pallas_call | solution.py:483
Async XLA Ops:
  0.0 1.0 copy-start
  1.2 22.3 %collective-permute-start = (bf16[512,256]{1,0:T(8,128)(2,1)S(1)}, bf16[512,256]{1,0:T(8,128)(2,1)S(1)}, u32[]{:S(2)}, u32[]{:S(2)}) collective-permute-start(bf16[512,256]{1,0:T(8,128)(2,1)S(1)} %get-tuple-element.25.chunk.refs_0_), channel_id=1, source_target_pairs={{0,24},{1,25},{2,26},{3,27},{4,28},{5,29},{6,30},{7,31},{8,0},{9,1... | collective-permute-start | bytes 786440 | tf_op jit(solution)/shard_map/ppermute | solution.py:21
  6.3 23.9 %collective-permute-start.1 = (bf16[512,256]{1,0:T(8,128)(2,1)S(1)}, bf16[512,256]{1,0:T(8,128)(2,1)S(1)}, u32[]{:S(2)}, u32[]{:S(2)}) collective-permute-start(bf16[512,256]{1,0:T(8,128)(2,1)S(1)} %get-tuple-element.26.chunk.refs_1_), channel_id=1, source_target_pairs={{0,24},{1,25},{2,26},{3,27},{4,28},{5,29},{6,30},{7,31},{8,0},{9,1... | collective-permute-start | bytes 786440 | tf_op jit(solution)/shard_map/ppermute | solution.py:21
  6.7 0.8 copy-start.1
  7.6 0.7 copy-start.2
  8.3 0.7 copy-start.3
  23.4 13.6 %collective-permute-start.2 = (bf16[512,256]{1,0:T(8,128)(2,1)S(1)}, bf16[512,256]{1,0:T(8,128)(2,1)S(1)}, u32[]{:S(2)}, u32[]{:S(2)}) collective-permute-start(bf16[512,256]{1,0:T(8,128)(2,1)S(1)} %collective-permute-done.chunk.refs_2_), channel_id=1, source_target_pairs={{0,24},{1,25},{2,26},{3,27},{4,28},{5,29},{6,30},{7,31},{8,0},{9,1... | collective-permute-start | bytes 786440 | tf_op jit(solution)/shard_map/ppermute | solution.py:21
  30.2 12.4 %collective-permute-start.3 = (bf16[512,256]{1,0:T(8,128)(2,1)S(1)}, bf16[512,256]{1,0:T(8,128)(2,1)S(1)}, u32[]{:S(2)}, u32[]{:S(2)}) collective-permute-start(bf16[512,256]{1,0:T(8,128)(2,1)S(1)} %collective-permute-done.1.chunk.refs_3_), channel_id=1, source_target_pairs={{0,24},{1,25},{2,26},{3,27},{4,28},{5,29},{6,30},{7,31},{8,0},{9,1... | collective-permute-start | bytes 786440 | tf_op jit(solution)/shard_map/ppermute | solution.py:21
  37.0 16.0 %collective-permute-start.4 = (bf16[512,256]{1,0:T(8,128)(2,1)S(1)}, bf16[512,256]{1,0:T(8,128)(2,1)S(1)}, u32[]{:S(2)}, u32[]{:S(2)}) collective-permute-start(bf16[512,256]{1,0:T(8,128)(2,1)S(1)} %collective-permute-done.2.chunk.refs_4_), channel_id=1, source_target_pairs={{0,24},{1,25},{2,26},{3,27},{4,28},{5,29},{6,30},{7,31},{8,0},{9,1... | collective-permute-start | bytes 786440 | tf_op jit(solution)/shard_map/ppermute | solution.py:21
  42.6 13.8 %collective-permute-start.5 = (bf16[512,256]{1,0:T(8,128)(2,1)S(1)}, bf16[512,256]{1,0:T(8,128)(2,1)S(1)}, u32[]{:S(2)}, u32[]{:S(2)}) collective-permute-start(bf16[512,256]{1,0:T(8,128)(2,1)S(1)} %collective-permute-done.3.chunk.refs_5_), channel_id=1, source_target_pairs={{0,24},{1,25},{2,26},{3,27},{4,28},{5,29},{6,30},{7,31},{8,0},{9,1... | collective-permute-start | bytes 786440 | tf_op jit(solution)/shard_map/ppermute | solution.py:21

commit v2 on v1

--- a/solution.py
+++ b/solution.py
@@ -54,6 +54,19 @@
         self.tail = self.heads * self.decode
         self.height = self.join * self.block + self.tail
         self.slots = groups * self.per_group
+        self.order = [0]
+        for hops in range(1, groups // 2 + 1):
+            self.order += [hops, groups - hops] if groups - hops > hops else [hops]
+
+    def source(self, distance):
+        return distance - 1 if distance <= self.groups // 2 else (distance + 1) % self.groups
+
+    def way(self, distance):
+        return -KV_HEADS if distance <= self.groups // 2 else KV_HEADS
+
+    def rank(self, distance):
+        near = jnp.where(distance > 0, 2 * distance - 1, 0)
+        return jnp.where(distance <= self.groups // 2, near, 2 * (self.groups - distance))
 
 
 def pack_kernel(plan, spans, *outs):
@@ -76,24 +89,27 @@
             slot = home[spans[j, me[0] * plan.requests + u]]
             group = lax.div(slot, plan.per_group)
             distance = lax.rem(group - me[0] + plan.groups, plan.groups)
-            chunk = distance * plan.per_group + slot - group * plan.per_group
+            chunk = plan.rank(distance) * plan.per_group + slot - group * plan.per_group
             count = work[chunk * stride] + 1
             work[chunk * stride] = count
             work[chunk * stride + count] = u * plan.join + j
             work[plan.slots * stride + u * plan.join + j] = chunk
 
 
-def prepare_kernel(plan, me, home, spans, newq_hbm, newkv_hbm, recomp, q_out, acc, places, turns, marks, fresh_k, fresh_v,
-                   last_kv, work, tok, newq, newkv, table, flat, tails, column, mask, sems):
-    loads = [pltpu.make_async_copy(newq_hbm, newq, sems.at[0]), pltpu.make_async_copy(newkv_hbm, newkv, sems.at[1])]
+def prepare_kernel(plan, me, home_hbm, spans_hbm, newq_hbm, newkv_hbm, recomp_hbm, q_out, acc, places, turns, marks,
+                   fresh_k, fresh_v, last_kv, work, home, spans, newq, newkv, recomp, table, flat, tails, column, mask, sems):
+    loads = [
+        pltpu.make_async_copy(source, target, sems.at[i])
+        for i, (source, target) in enumerate(
+            [(home_hbm, home), (spans_hbm, spans), (recomp_hbm, recomp), (newq_hbm, newq), (newkv_hbm, newkv)]
+        )
+    ]
     for load in loads:
         load.start()
-    plan_work(plan, me, home, spans, work)
     dim, fresh, requests, heads, block = plan.dim, plan.fresh, plan.requests, plan.heads, plan.block
     recomputed, decode, join = plan.recomputed, plan.decode, plan.join
     half = dim // 2
     scale = LOG2E / (dim**0.5)
-    tok[...] = jnp.zeros(tok.shape, jnp.float32)
 
     row = lax.broadcasted_iota(jnp.int32, (dim, dim), 0)
     rate = turns_per_step(lax.rem(row, half), dim)
@@ -101,15 +117,24 @@
     for j in range(join):
         turns[j] = sine_of_turns(rate * float(j * plan.length) + phase)
 
-    row = lax.broadcasted_iota(jnp.int32, (plan.height, dim), 0)
-    lane = lax.broadcasted_iota(jnp.int32, (plan.height, dim), 1)
-    counts = ((lane >= fresh) & (lane < 2 * fresh)) | ((row < block) & (lane == lax.rem(row, fresh)))
-    marks[...] = jnp.where(counts, 1.0, 0.0).astype(jnp.bfloat16)
-
-    row = lax.broadcasted_iota(jnp.int32, (plan.height, recomputed), 0)
-    key = lax.broadcasted_iota(jnp.int32, (plan.height, recomputed), 1)
-    reach = (row // block) * fresh + lax.rem(row, fresh)
-    mask[...] = jnp.where((row >= join * block) | (key <= reach), 0.0, -BIG)
+    number = lax.broadcasted_iota(jnp.int32, (fresh, dim), 0)
+    lane = lax.broadcasted_iota(jnp.int32, (fresh, dim), 1)
+    stale = (lane >= fresh) & (lane < 2 * fresh)
+    own = jnp.where(stale | (lane == number), 1.0, 0.0).astype(jnp.bfloat16)
+    other = jnp.where(stale, 1.0, 0.0).astype(jnp.bfloat16)
+    for head in range(heads):
+        marks[head * fresh : (head + 1) * fresh, :] = own
+    for first in range(block, plan.height - plan.tail, fresh):
+        marks[first : first + fresh, :] = other
+    marks[plan.height - plan.tail :, :] = other[: plan.tail]
+
+    number = lax.broadcasted_iota(jnp.int32, (fresh, recomputed), 0)
+    key = lax.broadcasted_iota(jnp.int32, (fresh, recomputed), 1)
+    for j in range(join):
+        seen = jnp.where(key <= j * fresh + number, 0.0, -BIG)
+        for head in range(heads):
+            mask[j * block + head * fresh : j * block + (head + 1) * fresh, :] = seen
+    mask[join * block :, :] = jnp.zeros((plan.tail, recomputed), jnp.float32)
 
     lane = lax.broadcasted_iota(jnp.int32, (fresh, dim), 1)
     rate = turns_per_step(lax.rem(lane, half), dim)
@@ -127,6 +152,9 @@
             table[1, u, j * fresh : (j + 1) * fresh, :] = sine_of_turns(at * signed)
         return carry
 
+    for load in loads[:3]:
+        load.wait()
+    plan_work(plan, me, home, spans, work)
     column[...] = jnp.zeros(column.shape, jnp.float32)
     lax.fori_loop(0, requests, places_of, 0)
     step = lax.broadcasted_iota(jnp.int32, (decode * requests, dim), 0) // requests
@@ -136,7 +164,7 @@
     last_cos = sine_of_turns(at * rate + 0.25)
     last_sin = sine_of_turns(at * jnp.where(lane < half, -rate, rate))
 
-    for load in loads:
+    for load in loads[3:]:
         load.wait()
 
     def queries_of(j, carry):
@@ -169,35 +197,35 @@
         jnp.bfloat16
     ).astype(jnp.float32)
     last_kv[:, dim:] = x[:, :, dim:].reshape(decode * requests, dim)
-    ones = jnp.ones((recomputed, dim), jnp.bfloat16)
     which = lax.rem(lax.broadcasted_iota(jnp.int32, (plan.tail, dim), 0), decode)
+    lead = lax.broadcasted_iota(jnp.int32, (plan.tail, dim), 1) == 0
 
     def fresh_of(u, carry):
         y = turn(flat[0, pl.ds(u, recomputed, stride=requests), :], table[0, u], table[1, u])
         fresh_k[u] = y.T.astype(jnp.bfloat16)
         fresh_v[u] = flat[1, pl.ds(u, recomputed, stride=requests), :].astype(jnp.bfloat16)
         s = jnp.dot(q_out[u], fresh_k[u], preferred_element_type=jnp.float32)
-        p = jnp.exp2(s + mask[...]).astype(jnp.bfloat16)
-        values = jnp.concatenate([fresh_v[u], ones], 1)
-        acc[u] = jnp.dot(p, values, preferred_element_type=jnp.float32)
+        p = jnp.exp2(s + mask[...])
+        acc[u, :, dim:] = p
+        acc[u, :, :dim] = jnp.dot(p.astype(jnp.bfloat16), fresh_v[u], preferred_element_type=jnp.float32)
         mine = q_out[u, join * block :, :].astype(jnp.float32)
         for d in range(decode):
             pair = last_kv[pl.ds(d * requests + u, 1), :]
             s = jnp.sum(mine * pair[:, :dim], 1, keepdims=True)
             p = jnp.where(which >= d, jnp.exp2(jnp.broadcast_to(s, which.shape)), 0.0)
-            p = p.astype(jnp.bfloat16).astype(jnp.float32)
             acc[u, join * block :, :dim] += p * pair[:, dim:]
-            acc[u, join * block :, dim:] += p
+            acc[u, join * block :, dim:] += jnp.where(lead, p, 0.0)
         return carry
 
-    lax.fori_loop(0, requests, fresh_of, 0)
+    for u in range(requests):
+        fresh_of(u, 0)
 
 
 def spread_chunk(plan, chunk, values):
     dim, piece = plan.dim, plan.piece
     for first in range(0, chunk.shape[0], piece):
-        values[first : first + dim, :dim] = chunk[first + dim : first + piece, :dim]
-        values[first + dim : first + piece, :dim] = chunk[first + dim : first + piece, dim:]
+        values[first : first + dim, :] = chunk[first + dim : first + piece, :dim]
+        values[first + dim : first + piece, :] = chunk[first + dim : first + piece, dim:]
 
 
 def shift_keys(plan, chunk, first_token, place, angles, keys):
@@ -218,12 +246,10 @@
         keys[dim + fresh : dim + 2 * fresh, columns] = jnp.where(token == place, -BIG, 0.0).astype(jnp.bfloat16)
 
 
-def chunk_kernel(plan, order, work, chunk, places, turns, marks, q, _, acc, tok, keys, values):
+def chunk_kernel(plan, order, _work, chunk, places, turns, marks, q, _acc, acc, work, keys, values):
     dim, block, join = plan.dim, plan.block, plan.join
-    tok[...] = jnp.zeros(tok.shape, jnp.float32)
     length = chunk.shape[0]
     keys[dim + 2 * plan.fresh :, :] = jnp.zeros((dim - 2 * plan.fresh, length), jnp.bfloat16)
-    values[:, dim:] = jnp.ones((length, dim), jnp.bfloat16)
     spread_chunk(plan, chunk, values)
     base = order * (plan.requests + 1)
 
@@ -243,8 +269,14 @@
                 left = jnp.concatenate([q[u, k * block :, :], marks[:count, :]], 1)
                 s = jnp.dot(left, keys[...], preferred_element_type=jnp.float32)
                 prepare(jnp.minimum(n + 1, plan.requests - 1))
-                p = jnp.exp2(s).astype(jnp.bfloat16)
-                acc[u, k * block :, :] += jnp.dot(p, values[...], preferred_element_type=jnp.float32)
+                p = jnp.exp2(s)
+                parts = [p[:, first : first + dim] for first in range(0, length, dim)]
+                while len(parts) > 1:
+                    parts = [sum(parts[i : i + 2]) for i in range(0, len(parts), 2)]
+                acc[u, k * block :, dim:] += parts[0]
+                acc[u, k * block :, :dim] += jnp.dot(
+                    p.astype(jnp.bfloat16), values[...], preferred_element_type=jnp.float32
+                )
 
         return carry
 
@@ -259,26 +291,34 @@
     dim, fresh, requests, heads, block = plan.dim, plan.fresh, plan.requests, plan.heads, plan.block
     recomputed, decode, join = plan.recomputed, plan.decode, plan.join
 
-    def put(u, source, seen):
-        least, most, odd = seen
+    def quotient(a, weight):
+        inverse = pl.reciprocal(weight, approx=True)
+        return a * (inverse * (2.0 - weight * inverse))
+
+    def put(u, j, source, seen):
+        after = []
         for head in range(heads):
             rows = slice(head * fresh, (head + 1) * fresh)
             a, weight = source(rows)
-            o = a / weight
-            least, most = jnp.minimum(least, weight), jnp.maximum(most, weight)
-            odd = odd + o * 0.0
-            flat[head, pl.ds(u, fresh, stride=requests), :] = o
-        return least, most, odd
+            o = quotient(a, weight)
+            flat[j, head, pl.ds(u, fresh, stride=requests), :] = o
+            least, most, every = seen[head]
+            after.append((jnp.minimum(least, weight), jnp.maximum(most, weight), every + o))
+        return after
 
     def put_tail(u, a, weight):
-        o = a / weight
+        o = quotient(a, weight)
         tails[pl.ds(u, plan.tail, stride=requests), :] = o
-        return weight, weight, o * 0.0
+        return weight, weight, o
+
+    def summed(u, start, count):
+        a = acc[u, start : start + count, :]
+        return a[:, :dim], jnp.sum(a[:, dim:], 1, keepdims=True)
 
     def write(j):
         rows = pl.ds(j * fresh, fresh)
         for head in range(heads):
-            x = flat[head].reshape(fresh, requests, dim)
+            x = flat[j, head].reshape(fresh, requests, dim)
             done[rows, :, head * dim : (head + 1) * dim] = x.astype(jnp.bfloat16)
         return rows
 
@@ -291,33 +331,32 @@
         rows = pl.ds(j * fresh, fresh) if j < join else pl.ds(recomputed, decode)
         return pltpu.make_async_copy(done.at[rows], out.at[rows], sems.at[j])
 
-    shape = (fresh, dim)
-    seen = (jnp.full(shape, 1.0, jnp.float32), jnp.full(shape, 1.0, jnp.float32), jnp.zeros(shape, jnp.float32))
-    tail_good = jnp.bool_(True)
-    for u in range(requests):
-        a = acc[u, join * block :, :]
-        least, most, odd = put_tail(u, a[:, :dim], a[:, dim:])
-        tail_good &= (jnp.min(least) > 2.0**-60) & (jnp.max(most) < 2.0**60) & (jnp.min(odd) == 0.0)
+    def fits(seen):
+        least, most, every = functools.reduce(
+            lambda x, y: (jnp.minimum(x[0], y[0]), jnp.maximum(x[1], y[1]), x[2] + y[2]), seen
+        )
+        good = jnp.where((least > 2.0**-60) & (most < 2.0**60) & (every - every == 0.0), 1.0, 0.0)
+        return jnp.min(good) > 0.5
+
+    one, none = jnp.ones((fresh, 1), jnp.float32), jnp.zeros((fresh, dim), jnp.float32)
+    clean = [(one, one, none)] * heads
+    ends = [put_tail(u, *summed(u, join * block, plan.tail)) for u in range(requests)]
     write_tail()
     send(join).start()
+    seen = clean
     for j in range(join):
         for u in range(requests):
-            source = lambda rows: (
-                acc[u, j * block + rows.start : j * block + rows.stop, :dim],
-                acc[u, j * block + rows.start : j * block + rows.stop, dim:],
-            )
-            seen = put(u, source, seen)
+            source = lambda rows: summed(u, j * block + rows.start, fresh)
+            seen = put(u, j, source, seen)
         write(j)
         send(j).start()
-    least, most, odd = seen
-    good = tail_good & (jnp.min(least) > 2.0**-60) & (jnp.max(most) < 2.0**60) & (jnp.min(odd) == 0.0)
+    good = fits(ends) & fits(seen)
     for j in range(join + 1):
         send(j).wait()
 
     @pl.when(jnp.logical_not(good))
     def _():
         keys[dim + 2 * fresh :, :] = jnp.zeros((dim - 2 * fresh, plan.length), jnp.bfloat16)
-        unseen = (jnp.full(shape, 1.0, jnp.float32), jnp.full(shape, 1.0, jnp.float32), jnp.zeros(shape, jnp.float32))
 
         def fold(rows, s, v):
             before = peak[rows, :]
@@ -355,7 +394,7 @@
                 mark = marks[:count, :] if k == j else marks[block : block + count, :]
                 left = jnp.concatenate([mine, mark], 1)
                 s = jnp.dot(left, keys[...], preferred_element_type=jnp.float32)
-                fold(every, s, values[:, :dim])
+                fold(every, s, values[...])
             if j == join:
                 which = lax.rem(lax.broadcasted_iota(jnp.int32, (count, dim), 0), decode)
                 for d in range(decode):
@@ -374,9 +413,9 @@
             def again(u, carry):
                 sums(u, j)
                 if j < join:
-                    put(u, lambda rows: (top[rows, :], total[rows, :]), unseen)
+                    put(u, j, lambda rows: (top[rows, :], total[rows, :1]), clean)
                 else:
-                    put_tail(u, top[: plan.tail, :], total[: plan.tail, :])
+                    put_tail(u, top[: plan.tail, :], total[: plan.tail, :1])
                 return carry
 
             lax.fori_loop(0, requests, again, 0)
@@ -400,7 +439,7 @@
     params = lambda mib: pltpu.CompilerParams(vmem_limit_bytes=mib * MIB)
     inside = lambda x: pltpu.with_memory_space_constraint(x, pltpu.VMEM)
     outside = lambda x: pltpu.with_memory_space_constraint(x, pltpu.HBM)
-    cost = lambda us: pl.CostEstimate(flops=int(us * 1.1e9), bytes_accessed=0, transcendentals=0)
+    cost = lambda us: pl.CostEstimate(flops=int(us * 2e7), bytes_accessed=0, transcendentals=0)
 
     packed = pl.pallas_call(
         functools.partial(pack_kernel, plan),
@@ -412,13 +451,17 @@
         name="pack",
     )(span_kv)
 
-    moving = [shifted(x, "store", -KV_HEADS) for x in packed] if groups > 1 else []
+    buffers = {(0, c): x for c, x in enumerate(packed)}
+
+    for after in plan.order[1:3]:
+        for c in range(plan.per_group):
+            buffers[after, c] = shifted(packed[c], "store", plan.way(after))
 
     spans = request_spans.T
 
-    token = pltpu.VMEM((8, 128), jnp.float32)
+    work_type = pltpu.SMEM((plan.slots * (requests + 1) + requests * join,), jnp.int32)
     acc_type = pltpu.VMEM((requests, plan.height, 2 * dim), jnp.float32)
-    q, acc, places, turns, marks, fresh_k, fresh_v, last_kv, work, tok = pl.pallas_call(
+    q, acc, places, turns, marks, fresh_k, fresh_v, last_kv, work = pl.pallas_call(
         functools.partial(prepare_kernel, plan),
         out_shape=[
             pltpu.VMEM((requests, plan.height, dim), jnp.bfloat16),
@@ -429,56 +472,61 @@
             pltpu.VMEM((requests, dim, plan.recomputed), jnp.bfloat16),
             pltpu.VMEM((requests, plan.recomputed, dim), jnp.bfloat16),
             pltpu.VMEM((plan.decode * requests, 2 * dim), jnp.float32),
-            pltpu.SMEM((plan.slots * (requests + 1) + requests * join,), jnp.int32),
-            token,
+            work_type,
         ],
-        in_specs=[smem] * 3 + [anywhere] * 2 + [vmem],
-        out_specs=[vmem] * 8 + [smem, vmem],
+        in_specs=[smem] + [anywhere] * 5,
+        out_specs=[vmem] * 8 + [smem],
         scratch_shapes=[
+            pltpu.SMEM(span_home.shape, jnp.int32),
+            pltpu.SMEM(spans.shape, jnp.int32),
             pltpu.VMEM((plan.rows, requests, new_q.shape[2]), jnp.bfloat16),
             pltpu.VMEM((plan.rows, requests, 2 * dim), jnp.bfloat16),
+            pltpu.VMEM(recomp_pos.shape, jnp.int32),
             pltpu.VMEM((2, requests, plan.recomputed, dim), jnp.float32),
             pltpu.VMEM((plan.heads, plan.recomputed * requests, dim), jnp.float32),
             pltpu.VMEM((plan.heads * plan.decode * requests, dim), jnp.float32),
             pltpu.VMEM((dim, dim), jnp.float32),
             pltpu.VMEM((plan.height, plan.recomputed), jnp.float32),
-            pltpu.SemaphoreType.DMA((2,)),
+            pltpu.SemaphoreType.DMA((5,)),
         ],
         compiler_params=params(20),
         cost_estimate=cost(6.0),
         name="prepare",
-    )(me, span_home, spans, outside(new_q.transpose(1, 0, 2)), outside(new_kv.transpose(1, 0, 2)), recomp_pos)
-    work = pltpu.with_memory_space_constraint(work, pltpu.SMEM)
-
-    def take(order, chunk, acc):
+    )(me, *map(outside, [span_home, spans, new_q.transpose(1, 0, 2), new_kv.transpose(1, 0, 2), recomp_pos]))
+    scalar = lambda x: pltpu.with_memory_space_constraint(x, pltpu.SMEM)
+
+    def take(order, chunk, acc, work):
         return pl.pallas_call(
             functools.partial(chunk_kernel, plan, order),
-            out_shape=[acc_type, token],
+            out_shape=[acc_type, work_type],
             in_specs=[smem] + [vmem] * 6,
-            out_specs=[vmem] * 2,
-            input_output_aliases={6: 0},
+            out_specs=[vmem, smem],
+            input_output_aliases={6: 0, 0: 1},
             scratch_shapes=[
                 pltpu.VMEM((2 * dim, plan.length), jnp.bfloat16),
-                pltpu.VMEM((plan.length, 2 * dim), jnp.bfloat16),
+                pltpu.VMEM((plan.length, dim), jnp.bfloat16),
             ],
             compiler_params=params(12),
             cost_estimate=cost(2.5),
             name="chunk",
-        )(work, *map(inside, [chunk, places, turns, marks, q, acc]))
-
-    def onward(k, tok):
-        if k + plan.per_group < plan.slots - plan.per_group:
-            held, tok = lax.optimization_barrier((buffers[plan.per_group + k], tok))
-            buffers.append(shifted(held, "store", -KV_HEADS))
-
-    buffers = list(packed) + moving
-    onward(0, tok)
-    for order in range(plan.slots):
-        acc, tok = take(order, buffers[order], acc)
-        if order < plan.per_group - 1:
-            onward(order + 1, tok)
-        elif order >= plan.per_group:
-            onward(order, tok)
+        )(scalar(work), *map(inside, [chunk, places, turns, marks, q, acc]))
+
+    def onward(distance, c, work):
+        for after in plan.order:
+            if distance > 0 and after > 0 and plan.source(after) == distance:
+                buffers[distance, c], work = lax.optimization_barrier((buffers[distance, c], work))
+                buffers[after, c] = shifted(buffers[distance, c], "store", plan.way(after))
+        return work
+
+    chunks = [(distance, c) for distance in plan.order for c in range(plan.per_group)]
+    first = plan.per_group
+    if groups > 1:
+        work = onward(*chunks[first], work)
+    for order, (distance, c) in enumerate(chunks):
+        acc, work = take(order, buffers[distance, c], acc, work)
+        if order > first:
+            work = onward(distance, c, work)
+    buffers = [buffers[chunk] for chunk in chunks]
 
     out = pl.pallas_call(
         functools.partial(finish_kernel, plan),
@@ -487,11 +535,11 @@
         out_specs=anywhere,
         scratch_shapes=[
             pltpu.VMEM((plan.rows, requests, new_q.shape[2]), jnp.bfloat16),
-            pltpu.VMEM((plan.heads, plan.fresh * requests, dim), jnp.float32),
+            pltpu.VMEM((join, plan.heads, plan.fresh * requests, dim), jnp.float32),
             pltpu.VMEM((plan.heads * plan.decode * requests, dim), jnp.float32),
             pltpu.VMEM((plan.length, 2 * dim), jnp.bfloat16),
             pltpu.VMEM((2 * dim, plan.length), jnp.bfloat16),
-            pltpu.VMEM((plan.length, 2 * dim), jnp.bfloat16),
+            pltpu.VMEM((plan.length, dim), jnp.bfloat16),
             pltpu.VMEM((plan.block, dim), jnp.float32),
             pltpu.VMEM((plan.block, dim), jnp.float32),
             pltpu.VMEM((plan.block, dim), jnp.float32),
@@ -501,7 +549,7 @@
         compiler_params=params(24),
         cost_estimate=cost(3.0),
         name="finish",
-    )(work, *buffers, *map(inside, [places, turns, marks, q, acc, fresh_k, fresh_v, last_kv]))
+    )(scalar(work), *buffers, *map(inside, [places, turns, marks, q, acc, fresh_k, fresh_v, last_kv]))
     return out.transpose(1, 0, 2)
 
 

time: 157 us -> 141 us (0.90); the launches traced: 160 us -> 142 us
  Pallas kernels: 134 us -> 124 us
  starting transfers between devices: 21 us -> 11.1 us
  waiting for transfers between devices: 1.73 us -> 5.27 us
  local copies, waits for them, and re-layouts: 3.22 us -> 1.04 us
    ppermute x6, starting transfers between devices: 21 us -> 11.1 us  [shifted(): lax.ppermute(value, axis, [(i, (i + by) % devices) for i in range(devices)])]
    pallas_call x8, Pallas kernels: 27.2 us -> 20.3 us  [take(): pl.pallas_call(functools.partial(chunk_kernel, plan, order), out_shape=[a...]
    ppermute x6, waiting for transfers between devices: 1.73 us -> 5.27 us  [shifted(): lax.ppermute(value, axis, [(i, (i + by) % devices) for i in range(devices)])]
    pallas_call x1, Pallas kernels: 10.5 us -> 7.54 us  [local(): pl.pallas_call(functools.partial(prepare_kernel, plan), out_shape=[pltpu....]
    unnamed x8 -> x2, local copies, waits for them, and re-layouts: 3.22 us -> 1.04 us
  transfers between devices with their start and end apart: 6 -> 6, of which waited for: 2 -> 3; matrix products, arithmetic and copies ran while one was open for 0% -> 0% of each run, Pallas kernels for 19% -> 16%
where the time goes in v2:
time: 141 us; the launch traced here: 142 us
  Pallas kernels  124 us (88%)
  starting transfers between devices  11.1 us (8%)
  waiting for transfers between devices  5.27 us (4%)
    pallas_call x1, Pallas kernels, local(): pl.pallas_call(functools.partial(finish_kernel, plan), out_shape=jax.Shap...  96.1 us
    pallas_call x8, Pallas kernels, take(): pl.pallas_call(functools.partial(chunk_kernel, plan, order), out_shape=[a...  20.3 us
    ppermute x6, starting transfers between devices, shifted(): lax.ppermute(value, axis, [(i, (i + by) % devices) for i in range(devices)])  11.1 us
    pallas_call x1, Pallas kernels, local(): pl.pallas_call(functools.partial(prepare_kernel, plan), out_shape=[pltpu....  7.54 us
    ppermute x6, waiting for transfers between devices, shifted(): lax.ppermute(value, axis, [(i, (i + by) % devices) for i in range(devices)])  5.27 us
  transfers between devices with their start and end apart: 6, of which 3 were waited for; matrix products, arithmetic and copies ran while one was open for 0% of the time, Pallas kernels for 16%

profile of v2, /device:TPU:0, one launch (start us, length us, event | category | flops | bytes accessed | tf_op | source)
XLA Modules:
  0.0 141.7 jit_solution(3919711902839265726)
XLA Ops:
  0.0 0.0 copy-start
  0.0 1.0 copy-done
  1.0 0.1 pack.1
  1.2 5.1 %collective-permute-start.1 = (bf16[512,256]{1,0:T(8,128)(2,1)S(1)}, bf16[512,256]{1,0:T(8,128)(2,1)S(1)}, u32[]{:S(2)}, u32[]{:S(2)}) collective-permute-start(bf16[512,256]{1,0:T(8,128)(2,1)S(1)} %get-tuple-element.37.chunk.refs_0_), channel_id=1, source_target_pairs={{0,24},{1,25},{2,26},{3,27},{4,28},{5,29},{6,30},{7,31},{8,0},{9,1... | collective-permute-start | bytes 786440 | tf_op jit(solution)/shard_map/ppermute | solution.py:21
  6.3 0.4 collective-permute-start
  6.7 1.6 %collective-permute-start.3 = (bf16[512,256]{1,0:T(8,128)(2,1)S(1)}, bf16[512,256]{1,0:T(8,128)(2,1)S(1)}, u32[]{:S(2)}, u32[]{:S(2)}) collective-permute-start(bf16[512,256]{1,0:T(8,128)(2,1)S(1)} %get-tuple-element.36.chunk.refs_1_), channel_id=1, source_target_pairs={{0,8},{1,9},{2,10},{3,11},{4,12},{5,13},{6,14},{7,15},{8,16},{9,17... | collective-permute-start | bytes 786440 | tf_op jit(solution)/shard_map/ppermute | solution.py:21
  8.3 0.0 collective-permute-start.2
  8.3 7.5 %prepare.1 = (bf16[8,1040,128]{2,1,0:T(8,128)(2,1)S(1)}, f32[8,1040,256]{2,1,0:T(8,128)S(1)}, f32[32,32,128]{2,1,0:T(8,128)S(1)}, f32[4,128,128]{2,1,0:T(8,128)S...) custom-call(s32[1]{0:T(128)} %bitcast.me, ...), custom_call_target="tpu_custom_call" | custom-call | flops 120000000 | tf_op jit(solution)/shard_map/prepare/pallas_call | solution.py:464
  15.9 0.0 collective-permute-done.1.chunk.refs_2_
  15.9 3.8 %collective-permute-start.4 = (bf16[512,256]{1,0:T(8,128)(2,1)S(1)}, bf16[512,256]{1,0:T(8,128)(2,1)S(1)}, u32[]{:S(2)}, u32[]{:S(2)}) collective-permute-start(bf16[512,256]{1,0:T(8,128)(2,1)S(1)} %collective-permute-done.1.chunk.refs_2_), channel_id=1, source_target_pairs={{0,24},{1,25},{2,26},{3,27},{4,28},{5,29},{6,30},{7,31},{8,0},{9,1... | collective-permute-start | bytes 786440 | tf_op jit(solution)/shard_map/ppermute | solution.py:21
  19.7 3.4 %chunk.8 = (f32[8,1040,256]{2,1,0:T(8,128)S(1)}, s32[104]{0:T(128)S(4)}) custom-call(s32[104]{0:T(128)S(4)} %get-tuple-element.39._work, bf16[512,256]{1,0:T(8,128)(2,1)S(1)} %get-tuple-element.37.chunk.refs_0_, f32[32,32,128]{2,1,0:T(8,128)S(1)} %get-tuple-element.40.places.refs_8_, ...), custom_call_target="tpu_custom_call", output_to_operand_aliasing={{0}: (6, {}), {1}: (0, {})} | custom-call | flops 50000000 | tf_op jit(solution)/shard_map/chunk/pallas_call | solution.py:499
  23.2 1.8 %chunk.9 = (f32[8,1040,256]{2,1,0:T(8,128)S(1)}, s32[104]{0:T(128)S(4)}) custom-call(s32[104]{0:T(128)S(4)} %get-tuple-element.45._work, bf16[512,256]{1,0:T(8,128)(2,1)S(1)} %get-tuple-element.36.chunk.refs_1_, f32[32,32,128]{2,1,0:T(8,128)S(1)} %get-tuple-element.40.places.refs_8_, ...), custom_call_target="tpu_custom_call", output_to_operand_aliasing={{0}: (6, {}), {1}: (0, {})} | custom-call | flops 50000000 | tf_op jit(solution)/shard_map/chunk/pallas_call | solution.py:499
  25.0 1.7 %chunk.10 = (f32[8,1040,256]{2,1,0:T(8,128)S(1)}, s32[104]{0:T(128)S(4)}) custom-call(s32[104]{0:T(128)S(4)} %get-tuple-element.47._work, bf16[512,256]{1,0:T(8,128)(2,1)S(1)} %collective-permute-done.1.chunk.refs_2_, f32[32,32,128]{2,1,0:T(8,128)S(1)} %get-tuple-element.40.places.refs_8_, ...), custom_call_target="tpu_custom_call", output_to_operand_aliasing={{0}: (6, {}), {1}: (0, {})} | custom-call | flops 50000000 | tf_op jit(solution)/shard_map/chunk/pallas_call | solution.py:499
  26.8 0.0 collective-permute-done.chunk.refs_3_
  26.8 2.5 %chunk.11 = (f32[8,1040,256]{2,1,0:T(8,128)S(1)}, s32[104]{0:T(128)S(4)}) custom-call(s32[104]{0:T(128)S(4)} %get-tuple-element.50._work, bf16[512,256]{1,0:T(8,128)(2,1)S(1)} %collective-permute-done.chunk.refs_3_, f32[32,32,128]{2,1,0:T(8,128)S(1)} %get-tuple-element.40.places.refs_8_, ...), custom_call_target="tpu_custom_call", output_to_operand_aliasing={{0}: (6, {}), {1}: (0, {})} | custom-call | flops 50000000 | tf_op jit(solution)/shard_map/chunk/pallas_call | solution.py:499
  29.3 0.1 collective-permute-start.5
  29.3 1.5 %collective-permute-done.2.chunk.refs_4_ = bf16[512,256]{1,0:T(8,128)(2,1)S(1)} collective-permute-done((bf16[512,256]{1,0:T(8,128)(2,1)S(1)}, bf16[512,256]{1,0:T(8,128)(2,1)S(1)}, u32[]{:S(2)}, u32[]{:S(2)}) %collective-permute-start.2) | collective-permute-done | bytes 262176 | tf_op jit(solution)/shard_map/ppermute | solution.py:21
  30.8 1.3 chunk.12
  32.1 0.0 collective-permute-done.3.chunk.refs_5_
  32.1 0.7 chunk.13
  32.8 2.7 %collective-permute-done.4.chunk.refs_6_ = bf16[512,256]{1,0:T(8,128)(2,1)S(1)} collective-permute-done((bf16[512,256]{1,0:T(8,128)(2,1)S(1)}, bf16[512,256]{1,0:T(8,128)(2,1)S(1)}, u32[]{:S(2)}, u32[]{:S(2)}) %collective-permute-start.4) | collective-permute-done | bytes 262176 | tf_op jit(solution)/shard_map/ppermute | solution.py:21
  35.5 3.4 %chunk.14 = (f32[8,1040,256]{2,1,0:T(8,128)S(1)}, s32[104]{0:T(128)S(4)}) custom-call(s32[104]{0:T(128)S(4)} %get-tuple-element.57._work, bf16[512,256]{1,0:T(8,128)(2,1)S(1)} %collective-permute-done.4.chunk.refs_6_, f32[32,32,128]{2,1,0:T(8,128)S(1)} %get-tuple-element.40.places.refs_8_, ...), custom_call_target="tpu_custom_call", output_to_operand_aliasing={{0}: (6, {}), {1}: (0, {})} | custom-call | flops 50000000 | tf_op jit(solution)/shard_map/chunk/pallas_call | solution.py:499
  38.9 1.1 collective-permute-done.5.chunk.refs_7_
  40.0 5.4 %chunk.15 = (f32[8,1040,256]{2,1,0:T(8,128)S(1)}, s32[104]{0:T(128)S(4)}) custom-call(s32[104]{0:T(128)S(4)} %get-tuple-element.59._work, bf16[512,256]{1,0:T(8,128)(2,1)S(1)} %collective-permute-done.5.chunk.refs_7_, f32[32,32,128]{2,1,0:T(8,128)S(1)} %get-tuple-element.40.places.refs_8_, ...), custom_call_target="tpu_custom_call", output_to_operand_aliasing={{0}: (6, {}), {1}: (0, {})} | custom-call | flops 50000000 | tf_op jit(solution)/shard_map/chunk/pallas_call | solution.py:499
  45.4 96.1 %finish.1 = bf16[130,8,1024]{2,1,0:T(8,128)(2,1)} custom-call(s32[104]{0:T(128)S(4)} %get-tuple-element.62.work, bf16[512,256]{1,0:T(8,128)(2,1)S(1)} %get-tuple-element.37.chunk.refs_0_, bf16[512,256]{1,0:T(8,128)(2,1)S(1)} %get-tuple-element.36.chunk.refs_1_, bf16[512,256]{1,0:T(8,128)(2,1)S(1)} %collective-permute-done.1.chunk.refs_2_, ...), custom_call_target="tpu_custom_call" | custom-call | flops 60000000 | tf_op jit(solution)/shard_map/finish/pallas_call | solution.py:531
Async XLA Ops:
  0.0 1.0 copy-start
  1.2 14.7 %collective-permute-start.1 = (bf16[512,256]{1,0:T(8,128)(2,1)S(1)}, bf16[512,256]{1,0:T(8,128)(2,1)S(1)}, u32[]{:S(2)}, u32[]{:S(2)}) collective-permute-start(bf16[512,256]{1,0:T(8,128)(2,1)S(1)} %get-tuple-element.37.chunk.refs_0_), channel_id=1, source_target_pairs={{0,24},{1,25},{2,26},{3,27},{4,28},{5,29},{6,30},{7,31},{8,0},{9,1... | collective-permute-start | bytes 786440 | tf_op jit(solution)/shard_map/ppermute | solution.py:21
  6.3 20.5 %collective-permute-start = (bf16[512,256]{1,0:T(8,128)(2,1)S(1)}, bf16[512,256]{1,0:T(8,128)(2,1)S(1)}, u32[]{:S(2)}, u32[]{:S(2)}) collective-permute-start(bf16[512,256]{1,0:T(8,128)(2,1)S(1)} %get-tuple-element.36.chunk.refs_1_), channel_id=1, source_target_pairs={{0,24},{1,25},{2,26},{3,27},{4,28},{5,29},{6,30},{7,31},{8,0},{9,1... | collective-permute-start | bytes 786440 | tf_op jit(solution)/shard_map/ppermute | solution.py:21
  6.7 25.3 %collective-permute-start.3 = (bf16[512,256]{1,0:T(8,128)(2,1)S(1)}, bf16[512,256]{1,0:T(8,128)(2,1)S(1)}, u32[]{:S(2)}, u32[]{:S(2)}) collective-permute-start(bf16[512,256]{1,0:T(8,128)(2,1)S(1)} %get-tuple-element.36.chunk.refs_1_), channel_id=1, source_target_pairs={{0,8},{1,9},{2,10},{3,11},{4,12},{5,13},{6,14},{7,15},{8,16},{9,17... | collective-permute-start | bytes 786440 | tf_op jit(solution)/shard_map/ppermute | solution.py:21
  8.3 22.5 %collective-permute-start.2 = (bf16[512,256]{1,0:T(8,128)(2,1)S(1)}, bf16[512,256]{1,0:T(8,128)(2,1)S(1)}, u32[]{:S(2)}, u32[]{:S(2)}) collective-permute-start(bf16[512,256]{1,0:T(8,128)(2,1)S(1)} %get-tuple-element.37.chunk.refs_0_), channel_id=1, source_target_pairs={{0,8},{1,9},{2,10},{3,11},{4,12},{5,13},{6,14},{7,15},{8,16},{9,17... | collective-permute-start | bytes 786440 | tf_op jit(solution)/shard_map/ppermute | solution.py:21
  15.9 19.6 %collective-permute-start.4 = (bf16[512,256]{1,0:T(8,128)(2,1)S(1)}, bf16[512,256]{1,0:T(8,128)(2,1)S(1)}, u32[]{:S(2)}, u32[]{:S(2)}) collective-permute-start(bf16[512,256]{1,0:T(8,128)(2,1)S(1)} %collective-permute-done.1.chunk.refs_2_), channel_id=1, source_target_pairs={{0,24},{1,25},{2,26},{3,27},{4,28},{5,29},{6,30},{7,31},{8,0},{9,1... | collective-permute-start | bytes 786440 | tf_op jit(solution)/shard_map/ppermute | solution.py:21
  29.3 10.7 %collective-permute-start.5 = (bf16[512,256]{1,0:T(8,128)(2,1)S(1)}, bf16[512,256]{1,0:T(8,128)(2,1)S(1)}, u32[]{:S(2)}, u32[]{:S(2)}) collective-permute-start(bf16[512,256]{1,0:T(8,128)(2,1)S(1)} %collective-permute-done.chunk.refs_3_), channel_id=1, source_target_pairs={{0,24},{1,25},{2,26},{3,27},{4,28},{5,29},{6,30},{7,31},{8,0},{9,1... | collective-permute-start | bytes 786440 | tf_op jit(solution)/shard_map/ppermute | solution.py:21

commit v3 on v2

--- a/solution.py
+++ b/solution.py
@@ -140,7 +140,7 @@
     rate = turns_per_step(lax.rem(lane, half), dim)
     signed = jnp.where(lane < half, -rate, rate)
 
-    def places_of(u, carry):
+    def places_of(u):
         request = me[0] * requests + u
         column[:join, :fresh] = recomp[request].astype(jnp.float32)
         upright = column[...].T
@@ -150,13 +150,13 @@
             at = inside + float(j * plan.length)
             table[0, u, j * fresh : (j + 1) * fresh, :] = sine_of_turns(at * rate + 0.25)
             table[1, u, j * fresh : (j + 1) * fresh, :] = sine_of_turns(at * signed)
-        return carry
 
     for load in loads[:3]:
         load.wait()
     plan_work(plan, me, home, spans, work)
     column[...] = jnp.zeros(column.shape, jnp.float32)
-    lax.fori_loop(0, requests, places_of, 0)
+    for u in range(requests):
+        places_of(u)
     step = lax.broadcasted_iota(jnp.int32, (decode * requests, dim), 0) // requests
     at = (join * plan.length + step).astype(jnp.float32)
     lane = lax.broadcasted_iota(jnp.int32, (decode * requests, dim), 1)
@@ -167,8 +167,8 @@
     for load in loads[3:]:
         load.wait()
 
-    def queries_of(j, carry):
-        rows = pl.ds(pl.multiple_of(j * fresh, fresh), fresh)
+    def queries_of(j):
+        rows = slice(j * fresh, (j + 1) * fresh)
         for head in range(heads):
             x = newq[rows, :, head * dim : (head + 1) * dim].astype(jnp.float32)
             flat[head, : fresh * requests, :] = x.reshape(fresh * requests, dim)
@@ -177,10 +177,10 @@
             sines = table[1, u, rows, :] * scale
             for head in range(heads):
                 y = turn(flat[head, pl.ds(u, fresh, stride=requests), :], cosines, sines)
-                q_out[u, pl.ds(pl.multiple_of(j * block + head * fresh, fresh), fresh), :] = y.astype(jnp.bfloat16)
-        return carry
-
-    lax.fori_loop(0, join, queries_of, 0)
+                q_out[u, pl.ds(j * block + head * fresh, fresh), :] = y.astype(jnp.bfloat16)
+
+    for j in range(join):
+        queries_of(j)
     for head in range(heads):
         x = newq[recomputed:, :, head * dim : (head + 1) * dim].astype(jnp.float32)
         y = turn(x.reshape(decode * requests, dim), last_cos, last_sin) * scale
@@ -200,7 +200,7 @@
     which = lax.rem(lax.broadcasted_iota(jnp.int32, (plan.tail, dim), 0), decode)
     lead = lax.broadcasted_iota(jnp.int32, (plan.tail, dim), 1) == 0
 
-    def fresh_of(u, carry):
+    def fresh_of(u):
         y = turn(flat[0, pl.ds(u, recomputed, stride=requests), :], table[0, u], table[1, u])
         fresh_k[u] = y.T.astype(jnp.bfloat16)
         fresh_v[u] = flat[1, pl.ds(u, recomputed, stride=requests), :].astype(jnp.bfloat16)
@@ -215,10 +215,9 @@
             p = jnp.where(which >= d, jnp.exp2(jnp.broadcast_to(s, which.shape)), 0.0)
             acc[u, join * block :, :dim] += p * pair[:, dim:]
             acc[u, join * block :, dim:] += jnp.where(lead, p, 0.0)
-        return carry
 
     for u in range(requests):
-        fresh_of(u, 0)
+        fresh_of(u)
 
 
 def spread_chunk(plan, chunk, values):
@@ -292,19 +291,25 @@
     recomputed, decode, join = plan.recomputed, plan.decode, plan.join
 
     def quotient(a, weight):
-        inverse = pl.reciprocal(weight, approx=True)
-        return a * (inverse * (2.0 - weight * inverse))
+        return a * pl.reciprocal(weight, approx=True)
+
+    def tree(join_two, items):
+        while len(items) > 1:
+            items = [functools.reduce(join_two, items[i : i + 2]) for i in range(0, len(items), 2)]
+        return items[0]
 
     def put(u, j, source, seen):
-        after = []
+        weights, quotients = [], []
         for head in range(heads):
-            rows = slice(head * fresh, (head + 1) * fresh)
-            a, weight = source(rows)
+            a, weight = source(slice(head * fresh, (head + 1) * fresh))
             o = quotient(a, weight)
             flat[j, head, pl.ds(u, fresh, stride=requests), :] = o
-            least, most, every = seen[head]
-            after.append((jnp.minimum(least, weight), jnp.maximum(most, weight), every + o))
-        return after
+            weights.append(weight)
+            quotients.append(o)
+        least, most, every = seen
+        least = jnp.minimum(least, tree(jnp.minimum, weights))
+        most = jnp.maximum(most, tree(jnp.maximum, weights))
+        return least, most, every + tree(jnp.add, quotients)
 
     def put_tail(u, a, weight):
         o = quotient(a, weight)
@@ -331,16 +336,14 @@
         rows = pl.ds(j * fresh, fresh) if j < join else pl.ds(recomputed, decode)
         return pltpu.make_async_copy(done.at[rows], out.at[rows], sems.at[j])
 
-    def fits(seen):
-        least, most, every = functools.reduce(
-            lambda x, y: (jnp.minimum(x[0], y[0]), jnp.maximum(x[1], y[1]), x[2] + y[2]), seen
-        )
-        good = jnp.where((least > 2.0**-60) & (most < 2.0**60) & (every - every == 0.0), 1.0, 0.0)
-        return jnp.min(good) > 0.5
+    def fits(least, most, every):
+        good = (least > 2.0**-60) & (most < 2.0**60) & (every - every == 0.0)
+        return jnp.min(jnp.where(good, 1.0, 0.0)) > 0.5
 
     one, none = jnp.ones((fresh, 1), jnp.float32), jnp.zeros((fresh, dim), jnp.float32)
-    clean = [(one, one, none)] * heads
+    clean = (one, one, none)
     ends = [put_tail(u, *summed(u, join * block, plan.tail)) for u in range(requests)]
+    ends = [tree(*pair) for pair in zip((jnp.minimum, jnp.maximum, jnp.add), map(list, zip(*ends)))]
     write_tail()
     send(join).start()
     seen = clean
@@ -350,7 +353,7 @@
             seen = put(u, j, source, seen)
         write(j)
         send(j).start()
-    good = fits(ends) & fits(seen)
+    good = fits(*ends) & fits(*seen)
     for j in range(join + 1):
         send(j).wait()
 

time: 141 us -> 139 us (0.986); the launches traced: 142 us -> 138 us
  Pallas kernels: 124 us -> 121 us
    pallas_call x1, Pallas kernels: 7.54 us -> 5.85 us  [local(): pl.pallas_call(functools.partial(prepare_kernel, plan), out_shape=[pltpu....]
  transfers between devices with their start and end apart: 6 -> 6, of which waited for: 3 -> 2; matrix products, arithmetic and copies ran while one was open for 0% -> 0% of each run, Pallas kernels for 16% -> 17%
where the time goes in v3:
time: 139 us; the launch traced here: 138 us
  Pallas kernels  121 us (87%)
  starting transfers between devices  11.1 us (8%)
  waiting for transfers between devices  3.92 us (3%)
    pallas_call x1, Pallas kernels, local(): pl.pallas_call(functools.partial(finish_kernel, plan), out_shape=jax.Shap...  95.1 us
    pallas_call x8, Pallas kernels, take(): pl.pallas_call(functools.partial(chunk_kernel, plan, order), out_shape=[a...  20.2 us
    ppermute x6, starting transfers between devices, shifted(): lax.ppermute(value, axis, [(i, (i + by) % devices) for i in range(devices)])  11.1 us
    pallas_call x1, Pallas kernels, local(): pl.pallas_call(functools.partial(prepare_kernel, plan), out_shape=[pltpu....  5.85 us
    ppermute x6, waiting for transfers between devices, shifted(): lax.ppermute(value, axis, [(i, (i + by) % devices) for i in range(devices)])  3.92 us
  transfers between devices with their start and end apart: 6, of which 2 were waited for; matrix products, arithmetic and copies ran while one was open for 0% of the time, Pallas kernels for 17%

profile of v3, /device:TPU:0, one launch (start us, length us, event | category | flops | bytes accessed | tf_op | source)
XLA Modules:
  0.0 137.7 jit_solution(17456101825538035371)
XLA Ops:
  0.0 0.0 copy-start
  0.0 1.0 copy-done
  1.0 0.1 pack.1
  1.2 5.1 %collective-permute-start.1 = (bf16[512,256]{1,0:T(8,128)(2,1)S(1)}, bf16[512,256]{1,0:T(8,128)(2,1)S(1)}, u32[]{:S(2)}, u32[]{:S(2)}) collective-permute-start(bf16[512,256]{1,0:T(8,128)(2,1)S(1)} %get-tuple-element.37.chunk.refs_0_), channel_id=1, source_target_pairs={{0,24},{1,25},{2,26},{3,27},{4,28},{5,29},{6,30},{7,31},{8,0},{9,1... | collective-permute-start | bytes 786440 | tf_op jit(solution)/shard_map/ppermute | solution.py:21
  6.3 0.4 collective-permute-start
  6.7 1.6 %collective-permute-start.3 = (bf16[512,256]{1,0:T(8,128)(2,1)S(1)}, bf16[512,256]{1,0:T(8,128)(2,1)S(1)}, u32[]{:S(2)}, u32[]{:S(2)}) collective-permute-start(bf16[512,256]{1,0:T(8,128)(2,1)S(1)} %get-tuple-element.36.chunk.refs_1_), channel_id=1, source_target_pairs={{0,8},{1,9},{2,10},{3,11},{4,12},{5,13},{6,14},{7,15},{8,16},{9,17... | collective-permute-start | bytes 786440 | tf_op jit(solution)/shard_map/ppermute | solution.py:21
  8.3 0.0 collective-permute-start.2
  8.3 5.8 %prepare.1 = (bf16[8,1040,128]{2,1,0:T(8,128)(2,1)S(1)}, f32[8,1040,256]{2,1,0:T(8,128)S(1)}, f32[32,32,128]{2,1,0:T(8,128)S(1)}, f32[4,128,128]{2,1,0:T(8,128)S...) custom-call(s32[1]{0:T(128)} %bitcast.me, ...), custom_call_target="tpu_custom_call" | custom-call | flops 120000000 | tf_op jit(solution)/shard_map/prepare/pallas_call | solution.py:467
  14.2 0.0 collective-permute-done.1.chunk.refs_2_
  14.2 3.8 %collective-permute-start.4 = (bf16[512,256]{1,0:T(8,128)(2,1)S(1)}, bf16[512,256]{1,0:T(8,128)(2,1)S(1)}, u32[]{:S(2)}, u32[]{:S(2)}) collective-permute-start(bf16[512,256]{1,0:T(8,128)(2,1)S(1)} %collective-permute-done.1.chunk.refs_2_), channel_id=1, source_target_pairs={{0,24},{1,25},{2,26},{3,27},{4,28},{5,29},{6,30},{7,31},{8,0},{9,1... | collective-permute-start | bytes 786440 | tf_op jit(solution)/shard_map/ppermute | solution.py:21
  18.1 0.5 chunk.8
  18.6 1.3 chunk.9
  19.9 3.1 %chunk.10 = (f32[8,1040,256]{2,1,0:T(8,128)S(1)}, s32[104]{0:T(128)S(4)}) custom-call(s32[104]{0:T(128)S(4)} %get-tuple-element.47._work, bf16[512,256]{1,0:T(8,128)(2,1)S(1)} %collective-permute-done.1.chunk.refs_2_, f32[32,32,128]{2,1,0:T(8,128)S(1)} %get-tuple-element.40.places.refs_8_, ...), custom_call_target="tpu_custom_call", output_to_operand_aliasing={{0}: (6, {}), {1}: (0, {})} | custom-call | flops 50000000 | tf_op jit(solution)/shard_map/chunk/pallas_call | solution.py:502
  22.9 0.0 collective-permute-done.chunk.refs_3_
  22.9 6.0 %chunk.11 = (f32[8,1040,256]{2,1,0:T(8,128)S(1)}, s32[104]{0:T(128)S(4)}) custom-call(s32[104]{0:T(128)S(4)} %get-tuple-element.50._work, bf16[512,256]{1,0:T(8,128)(2,1)S(1)} %collective-permute-done.chunk.refs_3_, f32[32,32,128]{2,1,0:T(8,128)S(1)} %get-tuple-element.40.places.refs_8_, ...), custom_call_target="tpu_custom_call", output_to_operand_aliasing={{0}: (6, {}), {1}: (0, {})} | custom-call | flops 50000000 | tf_op jit(solution)/shard_map/chunk/pallas_call | solution.py:502
  28.9 0.1 collective-permute-start.5
  29.0 1.8 %collective-permute-done.2.chunk.refs_4_ = bf16[512,256]{1,0:T(8,128)(2,1)S(1)} collective-permute-done((bf16[512,256]{1,0:T(8,128)(2,1)S(1)}, bf16[512,256]{1,0:T(8,128)(2,1)S(1)}, u32[]{:S(2)}, u32[]{:S(2)}) %collective-permute-start.2) | collective-permute-done | bytes 262176 | tf_op jit(solution)/shard_map/ppermute | solution.py:21
  30.8 2.4 %chunk.12 = (f32[8,1040,256]{2,1,0:T(8,128)S(1)}, s32[104]{0:T(128)S(4)}) custom-call(s32[104]{0:T(128)S(4)} %get-tuple-element.53._work, bf16[512,256]{1,0:T(8,128)(2,1)S(1)} %collective-permute-done.2.chunk.refs_4_, f32[32,32,128]{2,1,0:T(8,128)S(1)} %get-tuple-element.40.places.refs_8_, ...), custom_call_target="tpu_custom_call", output_to_operand_aliasing={{0}: (6, {}), {1}: (0, {})} | custom-call | flops 50000000 | tf_op jit(solution)/shard_map/chunk/pallas_call | solution.py:502
  33.2 0.0 collective-permute-done.3.chunk.refs_5_
  33.2 2.4 %chunk.13 = (f32[8,1040,256]{2,1,0:T(8,128)S(1)}, s32[104]{0:T(128)S(4)}) custom-call(s32[104]{0:T(128)S(4)} %get-tuple-element.55._work, bf16[512,256]{1,0:T(8,128)(2,1)S(1)} %collective-permute-done.3.chunk.refs_5_, f32[32,32,128]{2,1,0:T(8,128)S(1)} %get-tuple-element.40.places.refs_8_, ...), custom_call_target="tpu_custom_call", output_to_operand_aliasing={{0}: (6, {}), {1}: (0, {})} | custom-call | flops 50000000 | tf_op jit(solution)/shard_map/chunk/pallas_call | solution.py:502
  35.6 0.0 collective-permute-done.4.chunk.refs_6_
  35.6 2.2 %chunk.14 = (f32[8,1040,256]{2,1,0:T(8,128)S(1)}, s32[104]{0:T(128)S(4)}) custom-call(s32[104]{0:T(128)S(4)} %get-tuple-element.57._work, bf16[512,256]{1,0:T(8,128)(2,1)S(1)} %collective-permute-done.4.chunk.refs_6_, f32[32,32,128]{2,1,0:T(8,128)S(1)} %get-tuple-element.40.places.refs_8_, ...), custom_call_target="tpu_custom_call", output_to_operand_aliasing={{0}: (6, {}), {1}: (0, {})} | custom-call | flops 50000000 | tf_op jit(solution)/shard_map/chunk/pallas_call | solution.py:502
  37.9 2.1 %collective-permute-done.5.chunk.refs_7_ = bf16[512,256]{1,0:T(8,128)(2,1)S(1)} collective-permute-done((bf16[512,256]{1,0:T(8,128)(2,1)S(1)}, bf16[512,256]{1,0:T(8,128)(2,1)S(1)}, u32[]{:S(2)}, u32[]{:S(2)}) %collective-permute-start.5) | collective-permute-done | bytes 262176 | tf_op jit(solution)/shard_map/ppermute | solution.py:21
  40.0 2.4 %chunk.15 = (f32[8,1040,256]{2,1,0:T(8,128)S(1)}, s32[104]{0:T(128)S(4)}) custom-call(s32[104]{0:T(128)S(4)} %get-tuple-element.59._work, bf16[512,256]{1,0:T(8,128)(2,1)S(1)} %collective-permute-done.5.chunk.refs_7_, f32[32,32,128]{2,1,0:T(8,128)S(1)} %get-tuple-element.40.places.refs_8_, ...), custom_call_target="tpu_custom_call", output_to_operand_aliasing={{0}: (6, {}), {1}: (0, {})} | custom-call | flops 50000000 | tf_op jit(solution)/shard_map/chunk/pallas_call | solution.py:502
  42.4 95.1 %finish.1 = bf16[130,8,1024]{2,1,0:T(8,128)(2,1)} custom-call(s32[104]{0:T(128)S(4)} %get-tuple-element.62.work, bf16[512,256]{1,0:T(8,128)(2,1)S(1)} %get-tuple-element.37.chunk.refs_0_, bf16[512,256]{1,0:T(8,128)(2,1)S(1)} %get-tuple-element.36.chunk.refs_1_, bf16[512,256]{1,0:T(8,128)(2,1)S(1)} %collective-permute-done.1.chunk.refs_2_, ...), custom_call_target="tpu_custom_call" | custom-call | flops 60000000 | tf_op jit(solution)/shard_map/finish/pallas_call | solution.py:534
Async XLA Ops:
  0.0 1.0 copy-start
  1.2 13.0 %collective-permute-start.1 = (bf16[512,256]{1,0:T(8,128)(2,1)S(1)}, bf16[512,256]{1,0:T(8,128)(2,1)S(1)}, u32[]{:S(2)}, u32[]{:S(2)}) collective-permute-start(bf16[512,256]{1,0:T(8,128)(2,1)S(1)} %get-tuple-element.37.chunk.refs_0_), channel_id=1, source_target_pairs={{0,24},{1,25},{2,26},{3,27},{4,28},{5,29},{6,30},{7,31},{8,0},{9,1... | collective-permute-start | bytes 786440 | tf_op jit(solution)/shard_map/ppermute | solution.py:21
  6.3 16.6 %collective-permute-start = (bf16[512,256]{1,0:T(8,128)(2,1)S(1)}, bf16[512,256]{1,0:T(8,128)(2,1)S(1)}, u32[]{:S(2)}, u32[]{:S(2)}) collective-permute-start(bf16[512,256]{1,0:T(8,128)(2,1)S(1)} %get-tuple-element.36.chunk.refs_1_), channel_id=1, source_target_pairs={{0,24},{1,25},{2,26},{3,27},{4,28},{5,29},{6,30},{7,31},{8,0},{9,1... | collective-permute-start | bytes 786440 | tf_op jit(solution)/shard_map/ppermute | solution.py:21
  6.7 26.4 %collective-permute-start.3 = (bf16[512,256]{1,0:T(8,128)(2,1)S(1)}, bf16[512,256]{1,0:T(8,128)(2,1)S(1)}, u32[]{:S(2)}, u32[]{:S(2)}) collective-permute-start(bf16[512,256]{1,0:T(8,128)(2,1)S(1)} %get-tuple-element.36.chunk.refs_1_), channel_id=1, source_target_pairs={{0,8},{1,9},{2,10},{3,11},{4,12},{5,13},{6,14},{7,15},{8,16},{9,17... | collective-permute-start | bytes 786440 | tf_op jit(solution)/shard_map/ppermute | solution.py:21
  8.3 22.5 %collective-permute-start.2 = (bf16[512,256]{1,0:T(8,128)(2,1)S(1)}, bf16[512,256]{1,0:T(8,128)(2,1)S(1)}, u32[]{:S(2)}, u32[]{:S(2)}) collective-permute-start(bf16[512,256]{1,0:T(8,128)(2,1)S(1)} %get-tuple-element.37.chunk.refs_0_), channel_id=1, source_target_pairs={{0,8},{1,9},{2,10},{3,11},{4,12},{5,13},{6,14},{7,15},{8,16},{9,17... | collective-permute-start | bytes 786440 | tf_op jit(solution)/shard_map/ppermute | solution.py:21
  14.2 21.4 %collective-permute-start.4 = (bf16[512,256]{1,0:T(8,128)(2,1)S(1)}, bf16[512,256]{1,0:T(8,128)(2,1)S(1)}, u32[]{:S(2)}, u32[]{:S(2)}) collective-permute-start(bf16[512,256]{1,0:T(8,128)(2,1)S(1)} %collective-permute-done.1.chunk.refs_2_), channel_id=1, source_target_pairs={{0,24},{1,25},{2,26},{3,27},{4,28},{5,29},{6,30},{7,31},{8,0},{9,1... | collective-permute-start | bytes 786440 | tf_op jit(solution)/shard_map/ppermute | solution.py:21
  28.9 11.1 %collective-permute-start.5 = (bf16[512,256]{1,0:T(8,128)(2,1)S(1)}, bf16[512,256]{1,0:T(8,128)(2,1)S(1)}, u32[]{:S(2)}, u32[]{:S(2)}) collective-permute-start(bf16[512,256]{1,0:T(8,128)(2,1)S(1)} %collective-permute-done.chunk.refs_3_), channel_id=1, source_target_pairs={{0,24},{1,25},{2,26},{3,27},{4,28},{5,29},{6,30},{7,31},{8,0},{9,1... | collective-permute-start | bytes 786440 | tf_op jit(solution)/shard_map/ppermute | solution.py:21

commit v4 on v3

--- a/solution.py
+++ b/solution.py
@@ -191,7 +191,7 @@
 
     x = newkv[:recomputed, :, :].astype(jnp.float32)
     for side in range(2):
-        flat[side] = x[:, :, side * dim : (side + 1) * dim].reshape(recomputed * requests, dim)
+        flat[side, : recomputed * requests, :] = x[:, :, side * dim : (side + 1) * dim].reshape(recomputed * requests, dim)
     x = newkv[recomputed:, :, :].astype(jnp.float32)
     last_kv[:, :dim] = turn(x[:, :, :dim].reshape(decode * requests, dim), last_cos, last_sin).astype(
         jnp.bfloat16
@@ -323,7 +323,7 @@
     def write(j):
         rows = pl.ds(j * fresh, fresh)
         for head in range(heads):
-            x = flat[j, head].reshape(fresh, requests, dim)
+            x = flat[j, head, : fresh * requests, :].reshape(fresh, requests, dim)
             done[rows, :, head * dim : (head + 1) * dim] = x.astype(jnp.bfloat16)
         return rows
 
@@ -486,8 +486,8 @@
             pltpu.VMEM((plan.rows, requests, 2 * dim), jnp.bfloat16),
             pltpu.VMEM(recomp_pos.shape, jnp.int32),
             pltpu.VMEM((2, requests, plan.recomputed, dim), jnp.float32),
-            pltpu.VMEM((plan.heads, plan.recomputed * requests, dim), jnp.float32),
-            pltpu.VMEM((plan.heads * plan.decode * requests, dim), jnp.float32),
+            pltpu.VMEM((plan.heads, (plan.recomputed + 1) * requests, dim), jnp.float32),
+            pltpu.VMEM(((plan.tail + 1) * requests, dim), jnp.float32),
             pltpu.VMEM((dim, dim), jnp.float32),
             pltpu.VMEM((plan.height, plan.recomputed), jnp.float32),
             pltpu.SemaphoreType.DMA((5,)),
@@ -538,8 +538,8 @@
         out_specs=anywhere,
         scratch_shapes=[
             pltpu.VMEM((plan.rows, requests, new_q.shape[2]), jnp.bfloat16),
-            pltpu.VMEM((join, plan.heads, plan.fresh * requests, dim), jnp.float32),
-            pltpu.VMEM((plan.heads * plan.decode * requests, dim), jnp.float32),
+            pltpu.VMEM((join, plan.heads, (plan.fresh + 1) * requests, dim), jnp.float32),
+            pltpu.VMEM(((plan.tail + 1) * requests, dim), jnp.float32),
             pltpu.VMEM((plan.length, 2 * dim), jnp.bfloat16),
             pltpu.VMEM((2 * dim, plan.length), jnp.bfloat16),
             pltpu.VMEM((plan.length, dim), jnp.bfloat16),

time: 139 us -> 139 us (level)
  waiting for transfers between devices: 3.92 us -> 1.9 us
  starting transfers between devices: 11.1 us -> 12.7 us
    ppermute x6, waiting for transfers between devices: 3.92 us -> 1.9 us  [shifted(): lax.ppermute(value, axis, [(i, (i + by) % devices) for i in range(devices)])]
    ppermute x6, starting transfers between devices: 11.1 us -> 12.7 us  [shifted(): lax.ppermute(value, axis, [(i, (i + by) % devices) for i in range(devices)])]
  transfers between devices with their start and end apart: 6 -> 6, of which waited for: 2 -> 2; matrix products, arithmetic and copies ran while one was open for 0% -> 0% of each run, Pallas kernels for 17% -> 18%
where the time goes in v4:
time: 139 us; the launch traced here: 138 us
  Pallas kernels  122 us (88%)
  starting transfers between devices  12.7 us (9%)
  waiting for transfers between devices  1.9 us (1%)
    pallas_call x1, Pallas kernels, local(): pl.pallas_call(functools.partial(finish_kernel, plan), out_shape=jax.Shap...  95.5 us
    pallas_call x8, Pallas kernels, take(): pl.pallas_call(functools.partial(chunk_kernel, plan, order), out_shape=[a...  20.2 us
    ppermute x6, starting transfers between devices, shifted(): lax.ppermute(value, axis, [(i, (i + by) % devices) for i in range(devices)])  12.7 us
    pallas_call x1, Pallas kernels, local(): pl.pallas_call(functools.partial(prepare_kernel, plan), out_shape=[pltpu....  5.85 us
  transfers between devices with their start and end apart: 6, of which 2 were waited for; matrix products, arithmetic and copies ran while one was open for 0% of the time, Pallas kernels for 18%

profile of v4, /device:TPU:0, one launch (start us, length us, event | category | flops | bytes accessed | tf_op | source)
XLA Modules:
  0.0 137.6 jit_solution(2545037268797963395)
XLA Ops:
  0.0 0.0 copy-start
  0.0 1.0 copy-done
  1.0 0.1 pack.1
  1.2 5.1 %collective-permute-start.1 = (bf16[512,256]{1,0:T(8,128)(2,1)S(1)}, bf16[512,256]{1,0:T(8,128)(2,1)S(1)}, u32[]{:S(2)}, u32[]{:S(2)}) collective-permute-start(bf16[512,256]{1,0:T(8,128)(2,1)S(1)} %get-tuple-element.37.chunk.refs_0_), channel_id=1, source_target_pairs={{0,24},{1,25},{2,26},{3,27},{4,28},{5,29},{6,30},{7,31},{8,0},{9,1... | collective-permute-start | bytes 786440 | tf_op jit(solution)/shard_map/ppermute | solution.py:21
  6.3 0.4 collective-permute-start
  6.7 1.6 %collective-permute-start.3 = (bf16[512,256]{1,0:T(8,128)(2,1)S(1)}, bf16[512,256]{1,0:T(8,128)(2,1)S(1)}, u32[]{:S(2)}, u32[]{:S(2)}) collective-permute-start(bf16[512,256]{1,0:T(8,128)(2,1)S(1)} %get-tuple-element.36.chunk.refs_1_), channel_id=1, source_target_pairs={{0,8},{1,9},{2,10},{3,11},{4,12},{5,13},{6,14},{7,15},{8,16},{9,17... | collective-permute-start | bytes 786440 | tf_op jit(solution)/shard_map/ppermute | solution.py:21
  8.3 0.0 collective-permute-start.2
  8.3 5.9 %prepare.1 = (bf16[8,1040,128]{2,1,0:T(8,128)(2,1)S(1)}, f32[8,1040,256]{2,1,0:T(8,128)S(1)}, f32[32,32,128]{2,1,0:T(8,128)S(1)}, f32[4,128,128]{2,1,0:T(8,128)S...) custom-call(s32[1]{0:T(128)} %bitcast.me, ...), custom_call_target="tpu_custom_call" | custom-call | flops 120000000 | tf_op jit(solution)/shard_map/prepare/pallas_call | solution.py:467
  14.2 0.0 collective-permute-done.1.chunk.refs_2_
  14.2 3.8 %collective-permute-start.4 = (bf16[512,256]{1,0:T(8,128)(2,1)S(1)}, bf16[512,256]{1,0:T(8,128)(2,1)S(1)}, u32[]{:S(2)}, u32[]{:S(2)}) collective-permute-start(bf16[512,256]{1,0:T(8,128)(2,1)S(1)} %collective-permute-done.1.chunk.refs_2_), channel_id=1, source_target_pairs={{0,24},{1,25},{2,26},{3,27},{4,28},{5,29},{6,30},{7,31},{8,0},{9,1... | collective-permute-start | bytes 786440 | tf_op jit(solution)/shard_map/ppermute | solution.py:21
  18.1 2.0 %chunk.8 = (f32[8,1040,256]{2,1,0:T(8,128)S(1)}, s32[104]{0:T(128)S(4)}) custom-call(s32[104]{0:T(128)S(4)} %get-tuple-element.39._work, bf16[512,256]{1,0:T(8,128)(2,1)S(1)} %get-tuple-element.37.chunk.refs_0_, f32[32,32,128]{2,1,0:T(8,128)S(1)} %get-tuple-element.40.places.refs_8_, ...), custom_call_target="tpu_custom_call", output_to_operand_aliasing={{0}: (6, {}), {1}: (0, {})} | custom-call | flops 50000000 | tf_op jit(solution)/shard_map/chunk/pallas_call | solution.py:502
  20.1 5.1 %chunk.9 = (f32[8,1040,256]{2,1,0:T(8,128)S(1)}, s32[104]{0:T(128)S(4)}) custom-call(s32[104]{0:T(128)S(4)} %get-tuple-element.45._work, bf16[512,256]{1,0:T(8,128)(2,1)S(1)} %get-tuple-element.36.chunk.refs_1_, f32[32,32,128]{2,1,0:T(8,128)S(1)} %get-tuple-element.40.places.refs_8_, ...), custom_call_target="tpu_custom_call", output_to_operand_aliasing={{0}: (6, {}), {1}: (0, {})} | custom-call | flops 50000000 | tf_op jit(solution)/shard_map/chunk/pallas_call | solution.py:502
  25.2 2.5 %chunk.10 = (f32[8,1040,256]{2,1,0:T(8,128)S(1)}, s32[104]{0:T(128)S(4)}) custom-call(s32[104]{0:T(128)S(4)} %get-tuple-element.47._work, bf16[512,256]{1,0:T(8,128)(2,1)S(1)} %collective-permute-done.1.chunk.refs_2_, f32[32,32,128]{2,1,0:T(8,128)S(1)} %get-tuple-element.40.places.refs_8_, ...), custom_call_target="tpu_custom_call", output_to_operand_aliasing={{0}: (6, {}), {1}: (0, {})} | custom-call | flops 50000000 | tf_op jit(solution)/shard_map/chunk/pallas_call | solution.py:502
  27.7 0.0 collective-permute-done.chunk.refs_3_
  27.7 2.1 %chunk.11 = (f32[8,1040,256]{2,1,0:T(8,128)S(1)}, s32[104]{0:T(128)S(4)}) custom-call(s32[104]{0:T(128)S(4)} %get-tuple-element.50._work, bf16[512,256]{1,0:T(8,128)(2,1)S(1)} %collective-permute-done.chunk.refs_3_, f32[32,32,128]{2,1,0:T(8,128)S(1)} %get-tuple-element.40.places.refs_8_, ...), custom_call_target="tpu_custom_call", output_to_operand_aliasing={{0}: (6, {}), {1}: (0, {})} | custom-call | flops 50000000 | tf_op jit(solution)/shard_map/chunk/pallas_call | solution.py:502
  29.8 1.7 %collective-permute-start.5 = (bf16[512,256]{1,0:T(8,128)(2,1)S(1)}, bf16[512,256]{1,0:T(8,128)(2,1)S(1)}, u32[]{:S(2)}, u32[]{:S(2)}) collective-permute-start(bf16[512,256]{1,0:T(8,128)(2,1)S(1)} %collective-permute-done.chunk.refs_3_), channel_id=1, source_target_pairs={{0,24},{1,25},{2,26},{3,27},{4,28},{5,29},{6,30},{7,31},{8,0},{9,1... | collective-permute-start | bytes 786440 | tf_op jit(solution)/shard_map/ppermute | solution.py:21
  31.4 0.0 collective-permute-done.2.chunk.refs_4_
  31.4 3.2 %chunk.12 = (f32[8,1040,256]{2,1,0:T(8,128)S(1)}, s32[104]{0:T(128)S(4)}) custom-call(s32[104]{0:T(128)S(4)} %get-tuple-element.53._work, bf16[512,256]{1,0:T(8,128)(2,1)S(1)} %collective-permute-done.2.chunk.refs_4_, f32[32,32,128]{2,1,0:T(8,128)S(1)} %get-tuple-element.40.places.refs_8_, ...), custom_call_target="tpu_custom_call", output_to_operand_aliasing={{0}: (6, {}), {1}: (0, {})} | custom-call | flops 50000000 | tf_op jit(solution)/shard_map/chunk/pallas_call | solution.py:502
  34.7 0.0 collective-permute-done.3.chunk.refs_5_
  34.7 0.7 chunk.13
  35.4 0.1 collective-permute-done.4.chunk.refs_6_
  35.5 2.7 %chunk.14 = (f32[8,1040,256]{2,1,0:T(8,128)S(1)}, s32[104]{0:T(128)S(4)}) custom-call(s32[104]{0:T(128)S(4)} %get-tuple-element.57._work, bf16[512,256]{1,0:T(8,128)(2,1)S(1)} %collective-permute-done.4.chunk.refs_6_, f32[32,32,128]{2,1,0:T(8,128)S(1)} %get-tuple-element.40.places.refs_8_, ...), custom_call_target="tpu_custom_call", output_to_operand_aliasing={{0}: (6, {}), {1}: (0, {})} | custom-call | flops 50000000 | tf_op jit(solution)/shard_map/chunk/pallas_call | solution.py:502
  38.2 1.8 %collective-permute-done.5.chunk.refs_7_ = bf16[512,256]{1,0:T(8,128)(2,1)S(1)} collective-permute-done((bf16[512,256]{1,0:T(8,128)(2,1)S(1)}, bf16[512,256]{1,0:T(8,128)(2,1)S(1)}, u32[]{:S(2)}, u32[]{:S(2)}) %collective-permute-start.5) | collective-permute-done | bytes 262176 | tf_op jit(solution)/shard_map/ppermute | solution.py:21
  40.0 1.9 %chunk.15 = (f32[8,1040,256]{2,1,0:T(8,128)S(1)}, s32[104]{0:T(128)S(4)}) custom-call(s32[104]{0:T(128)S(4)} %get-tuple-element.59._work, bf16[512,256]{1,0:T(8,128)(2,1)S(1)} %collective-permute-done.5.chunk.refs_7_, f32[32,32,128]{2,1,0:T(8,128)S(1)} %get-tuple-element.40.places.refs_8_, ...), custom_call_target="tpu_custom_call", output_to_operand_aliasing={{0}: (6, {}), {1}: (0, {})} | custom-call | flops 50000000 | tf_op jit(solution)/shard_map/chunk/pallas_call | solution.py:502
  41.9 95.5 %finish.1 = bf16[130,8,1024]{2,1,0:T(8,128)(2,1)} custom-call(s32[104]{0:T(128)S(4)} %get-tuple-element.62.work, bf16[512,256]{1,0:T(8,128)(2,1)S(1)} %get-tuple-element.37.chunk.refs_0_, bf16[512,256]{1,0:T(8,128)(2,1)S(1)} %get-tuple-element.36.chunk.refs_1_, bf16[512,256]{1,0:T(8,128)(2,1)S(1)} %collective-permute-done.1.chunk.refs_2_, ...), custom_call_target="tpu_custom_call" | custom-call | flops 60000000 | tf_op jit(solution)/shard_map/finish/pallas_call | solution.py:534
Async XLA Ops:
  0.0 1.0 copy-start
  1.2 13.0 %collective-permute-start.1 = (bf16[512,256]{1,0:T(8,128)(2,1)S(1)}, bf16[512,256]{1,0:T(8,128)(2,1)S(1)}, u32[]{:S(2)}, u32[]{:S(2)}) collective-permute-start(bf16[512,256]{1,0:T(8,128)(2,1)S(1)} %get-tuple-element.37.chunk.refs_0_), channel_id=1, source_target_pairs={{0,24},{1,25},{2,26},{3,27},{4,28},{5,29},{6,30},{7,31},{8,0},{9,1... | collective-permute-start | bytes 786440 | tf_op jit(solution)/shard_map/ppermute | solution.py:21
  6.3 21.4 %collective-permute-start = (bf16[512,256]{1,0:T(8,128)(2,1)S(1)}, bf16[512,256]{1,0:T(8,128)(2,1)S(1)}, u32[]{:S(2)}, u32[]{:S(2)}) collective-permute-start(bf16[512,256]{1,0:T(8,128)(2,1)S(1)} %get-tuple-element.36.chunk.refs_1_), channel_id=1, source_target_pairs={{0,24},{1,25},{2,26},{3,27},{4,28},{5,29},{6,30},{7,31},{8,0},{9,1... | collective-permute-start | bytes 786440 | tf_op jit(solution)/shard_map/ppermute | solution.py:21
  6.7 27.9 %collective-permute-start.3 = (bf16[512,256]{1,0:T(8,128)(2,1)S(1)}, bf16[512,256]{1,0:T(8,128)(2,1)S(1)}, u32[]{:S(2)}, u32[]{:S(2)}) collective-permute-start(bf16[512,256]{1,0:T(8,128)(2,1)S(1)} %get-tuple-element.36.chunk.refs_1_), channel_id=1, source_target_pairs={{0,8},{1,9},{2,10},{3,11},{4,12},{5,13},{6,14},{7,15},{8,16},{9,17... | collective-permute-start | bytes 786440 | tf_op jit(solution)/shard_map/ppermute | solution.py:21
  8.3 23.1 %collective-permute-start.2 = (bf16[512,256]{1,0:T(8,128)(2,1)S(1)}, bf16[512,256]{1,0:T(8,128)(2,1)S(1)}, u32[]{:S(2)}, u32[]{:S(2)}) collective-permute-start(bf16[512,256]{1,0:T(8,128)(2,1)S(1)} %get-tuple-element.37.chunk.refs_0_), channel_id=1, source_target_pairs={{0,8},{1,9},{2,10},{3,11},{4,12},{5,13},{6,14},{7,15},{8,16},{9,17... | collective-permute-start | bytes 786440 | tf_op jit(solution)/shard_map/ppermute | solution.py:21
  14.2 21.3 %collective-permute-start.4 = (bf16[512,256]{1,0:T(8,128)(2,1)S(1)}, bf16[512,256]{1,0:T(8,128)(2,1)S(1)}, u32[]{:S(2)}, u32[]{:S(2)}) collective-permute-start(bf16[512,256]{1,0:T(8,128)(2,1)S(1)} %collective-permute-done.1.chunk.refs_2_), channel_id=1, source_target_pairs={{0,24},{1,25},{2,26},{3,27},{4,28},{5,29},{6,30},{7,31},{8,0},{9,1... | collective-permute-start | bytes 786440 | tf_op jit(solution)/shard_map/ppermute | solution.py:21
  29.8 10.2 %collective-permute-start.5 = (bf16[512,256]{1,0:T(8,128)(2,1)S(1)}, bf16[512,256]{1,0:T(8,128)(2,1)S(1)}, u32[]{:S(2)}, u32[]{:S(2)}) collective-permute-start(bf16[512,256]{1,0:T(8,128)(2,1)S(1)} %collective-permute-done.chunk.refs_3_), channel_id=1, source_target_pairs={{0,24},{1,25},{2,26},{3,27},{4,28},{5,29},{6,30},{7,31},{8,0},{9,1... | collective-permute-start | bytes 786440 | tf_op jit(solution)/shard_map/ppermute | solution.py:21
